TPU v7x, 128 devices: a whole 4x4x4 slice. The times are simulated.
128 devices in a mesh: row: 32 (over y, z, core), col: 4 (over x).
Axes of the slice: x: 4, y: 4, z: 4, core: 2. Of those that a mesh axis runs over, the one named last changes fastest.
Arguments:
- hidden_in: bfloat16 [4096, 24576], P('row'), may hold values from -6 to 6
- down_weight: bfloat16 [24576, 6144], P('row', 'col'), may hold values from -0.0390625 to 0.0390625
- out_grad: bfloat16 [4096, 6144], P('row', 'col'), may hold values from -6 to 6
Outputs:
- ffn_out: bfloat16 [4096, 6144], P('row', 'col')
- hidden_grad: bfloat16 [4096, 24576], P('col', 'row')
- weight_grad: bfloat16 [24576, 6144], P('row', 'col')
All inputs are finite; a program needn't handle non-finite values.
Results may differ from a plain program's by a relative error of at most 0.024.
Values may be sent and summed in bfloat16 or wider, within the bound.
No kernel may reach another device: no remote copies, remote signals or barrier semaphores. Data moves between devices by JAX's collectives and lax.ppermute only.
A program may use at most 128 MiB of HBM per device.

v0:
```python
import functools

import jax
import jax.numpy as jnp
from jax import lax
from jax.experimental import pallas as pl
from jax.experimental.pallas import tpu as pltpu
from jax.sharding import Mesh, PartitionSpec as P

gelu_coeff = 0.7978845608
cubic_coeff = 0.044715


def gelu_value(inputs):
    inner = gelu_coeff * (inputs + cubic_coeff * inputs * inputs * inputs)
    return 0.5 * inputs * (1.0 + jnp.tanh(inner))


def gelu_slope(inputs):
    tanh_part = jnp.tanh(gelu_coeff * (inputs + cubic_coeff * inputs * inputs * inputs))
    return 0.5 * (1.0 + tanh_part) + 0.5 * inputs * (1.0 - tanh_part * tanh_part) * gelu_coeff * (
        1.0 + 3.0 * cubic_coeff * inputs * inputs
    )


RIGHT = [(i, (i + 1) % 4) for i in range(4)]
LEFT = [(i, (i + 3) % 4) for i in range(4)]
SWAP = [(0, 1), (1, 0)]
f32 = jnp.float32
bf16 = jnp.bfloat16


def tie(*values):
    return lax.optimization_barrier(values)


def shift(block, axis):
    return tie(lax.ppermute(block, axis, RIGHT), lax.ppermute(block, axis, LEFT))


def relay(left, right, axis):
    half = left.shape[0] // 2
    return tie(lax.ppermute(left[:half], axis, RIGHT), lax.ppermute(right[half:], axis, LEFT))


def place(blocks, axis, dim):
    me = lax.axis_index(axis)
    shape = blocks[0].shape
    out = jnp.zeros(shape[:dim] + (4,) + shape[dim:], blocks[0].dtype)
    for block, by in zip(blocks, (0, 3, 1, 2)):
        at = [0] * out.ndim
        at[dim] = lax.rem(me + by, 4)
        out = lax.dynamic_update_slice(out, jnp.expand_dims(block, dim), at)
    return out


def at(part, index, dim):
    return lax.dynamic_index_in_dim(part, index, dim, keepdims=False)


def add(one, other):
    return (one.astype(f32) + other.astype(f32)).astype(bf16)


def split_kernel(x_ref, rows_ref, out_ref):
    group, _, width = out_ref.shape
    for chip in range(group):
        out_ref[chip] = rows_ref[:, chip * width : (chip + 1) * width]


def split_quarter(hidden_in, x, chips):
    tok, ff_all = hidden_in.shape
    sub, ff, steps = tok // 4, ff_all // chips, 4
    return pl.pallas_call(
        split_kernel,
        grid_spec=pltpu.PrefetchScalarGridSpec(
            num_scalar_prefetch=1,
            grid=(steps,),
            in_specs=[pl.BlockSpec((sub, ff_all // steps), lambda step, x_ref: (x_ref[0], step))],
            out_specs=pl.BlockSpec((chips // steps, sub, ff), lambda step, x_ref: (step, 0, 0)),
        ),
        out_shape=jax.ShapeDtypeStruct((chips, sub, ff), hidden_in.dtype),
        name="split_quarter",
    )(x.astype(jnp.int32).reshape(1), hidden_in)


def weight_kernel(scale, at_ref, act_0, act_1, act_2, act_3, grad_0, grad_1, *rest):
    *other, out_ref, act, grad, total = rest
    pair = pl.program_id(0)
    rows = act_0.shape[0]

    @pl.when(pair == 0)
    def _():
        act[:rows] = act_0[...]
        act[rows:] = act_1[...]

    @pl.when(pair == 1)
    def _():
        act[:rows] = act_2[...]
        act[rows:] = act_3[...]

    grad[:rows] = grad_0[...].reshape(rows, grad.shape[1])
    grad[rows:] = grad_1[...].reshape(rows, grad.shape[1])
    term = lax.dot_general(act[...], grad[...], (((0,), (0,)), ((), ())), preferred_element_type=f32)

    @pl.when(pair == 0)
    def _():
        total[...] = term

    @pl.when(pair == 1)
    def _():
        done = total[...] + term
        for ref in other:
            done = (done + ref[...].astype(f32)) * scale
        out_ref[...] = done.astype(out_ref.dtype)


def weight_sum(acts, places, grad_all, side, other=(), scale=1.0):
    rows, ff = acts[0].shape
    chips, _, sub, cols = grad_all.shape
    whole = pl.BlockSpec((ff // 2, cols), lambda pair, at_ref: (0, 0))
    act_spec = pl.BlockSpec((rows, ff // 2), lambda pair, at_ref: (0, at_ref[4]))
    grad_specs = [
        pl.BlockSpec((chips, 1, sub, cols), lambda pair, at_ref, which=which: (0, at_ref[2 * pair + which], 0, 0))
        for which in (0, 1)
    ]
    return pl.pallas_call(
        functools.partial(weight_kernel, scale),
        grid_spec=pltpu.PrefetchScalarGridSpec(
            num_scalar_prefetch=1,
            grid=(2,),
            in_specs=[act_spec] * 4 + grad_specs + [whole] * len(other),
            out_specs=whole,
            scratch_shapes=[
                pltpu.VMEM((2 * rows, ff // 2), bf16),
                pltpu.VMEM((2 * rows, cols), bf16),
                pltpu.VMEM((ff // 2, cols), f32),
            ],
        ),
        out_shape=jax.ShapeDtypeStruct((ff // 2, cols), bf16),
        compiler_params=pltpu.CompilerParams(vmem_limit_bytes=48 * 2**20),
        cost_estimate=pl.CostEstimate(
            flops=4 * rows * ff * cols, bytes_accessed=4 * rows * (ff + 2 * cols) + 2 * ff * cols, transcendentals=0
        ),
        name="weight_sum",
    )(jnp.stack([*places, side]).astype(jnp.int32), *acts, grad_all, grad_all, *other)


def body(hidden_in, down_weight, out_grad):
    tok, ff_all = hidden_in.shape
    ff_dev, cols = down_weight.shape
    ff = 2 * ff_dev
    sub = tok // 4
    x = lax.axis_index("x")
    core = lax.axis_index("core")
    plane = ("y", "z")

    mine = split_quarter(hidden_in, x, 16)
    mine, out_grad = tie(mine, out_grad)
    mine = lax.all_to_all(mine, plane, split_axis=0, concat_axis=0, tiled=True)
    mine = mine.reshape(4, 4, sub, ff)

    left_z, right_z = shift(out_grad, "z")
    far_z = jnp.concatenate(relay(left_z, right_z, "z"))
    line = place((out_grad, left_z, right_z, far_z), "z", 0)
    other_weight = lax.ppermute(down_weight, "core", SWAP)
    _, line, other_weight = tie(mine, line, other_weight)

    def activate(hidden):
        (act,) = tie(gelu_value(hidden.astype(f32)).astype(bf16))
        return act

    def forward(act):
        out = jnp.dot(act.reshape(16 * sub, ff), weight, preferred_element_type=f32)
        (out,) = tie(out.astype(bf16))
        return out.reshape(16, 1, sub, cols)

    def backward(grad):
        grad = grad.reshape(4 * tok, cols)
        out = lax.dot_general(grad, weight, (((1,), (1,)), ((), ())), preferred_element_type=f32)
        (out,) = tie(out.astype(bf16))
        return out.reshape(2, 2 * tok, ff)

    def exchange(terms):
        return lax.all_to_all(terms, plane, split_axis=0, concat_axis=0, tiled=True)

    places = [lax.rem(x + by, 4) for by in (0, 3, 1, 2)]

    def with_rows(rows, chunk, j):
        return lax.dynamic_update_slice(rows, at(chunk, x, 0)[:, None], (0, j, 0, 0))

    left, right = shift(mine, "x")
    left_y, right_y = shift(line, "y")
    weight = jnp.where(
        core == 0,
        jnp.concatenate([down_weight, other_weight]),
        jnp.concatenate([other_weight, down_weight]),
    )
    (weight,) = tie(weight)
    act_mine = activate(mine)
    part_mine = forward(act_mine)
    rows = with_rows(jnp.zeros((4, 4, sub, ff), bf16), mine, places[0])
    left, right, left_y, right_y, part_mine, act_mine, weight, rows = tie(
        left, right, left_y, right_y, part_mine, act_mine, weight, rows
    )

    far = relay(left, right, "x")
    far_y = relay(left_y, right_y, "y")
    act_left, act_right = activate(left), activate(right)
    terms_a = jnp.concatenate([part_mine, forward(act_left)], axis=1)
    part_right = forward(act_right)
    rows = with_rows(with_rows(rows, left, places[1]), right, places[2])
    far, far_y, terms_a, part_right, act_left, act_right, rows = lax.optimization_barrier(
        (far, far_y, terms_a, part_right, act_left, act_right, rows)
    )

    terms_a = exchange(terms_a)
    grad_all = place((line, left_y, right_y, jnp.concatenate(far_y)), "y", 0)
    quarter = lambda grad, by: backward(at(grad, lax.rem(x + by, 4), 0))
    opposite = quarter(grad_all, 2)
    opposite, grad_all, far = lax.optimization_barrier((opposite, grad_all, far))
    first, second = tie(lax.ppermute(opposite[0], "x", RIGHT), lax.ppermute(opposite[1], "x", LEFT))
    to_right, to_left = quarter(grad_all, 1), quarter(grad_all, 3)
    far = jnp.concatenate(far)
    act_far = activate(far)
    terms_b = jnp.concatenate([part_right, forward(act_far)], axis=1)
    rows = with_rows(rows, far, places[3])
    first, second, to_right, to_left, terms_b, act_far, grad_late, rows = tie(
        first, second, to_right, to_left, terms_b, act_far, grad_all, rows
    )

    sum_right, sum_left = add(to_right[0], first), add(to_left[1], second)
    sum_right, sum_left = tie(lax.ppermute(sum_right, "x", RIGHT), lax.ppermute(sum_left, "x", LEFT))
    terms_b = exchange(terms_b)
    home = quarter(grad_late, 0)
    acts = [act.reshape(16 * sub, ff) for act in (act_mine, act_left, act_right, act_far)]
    terms_a, other_core = tie(terms_a, 1 - core)
    give_sum = weight_sum(acts, places, grad_late.reshape(16, 4, sub, cols), other_core)
    sum_right, sum_left, to_right, to_left, grad_late, home, give_sum = lax.optimization_barrier(
        (sum_right, sum_left, to_right[1], to_left[0], grad_late, home, give_sum)
    )

    term_right, term_left = tie(lax.ppermute(to_right, "x", RIGHT), lax.ppermute(to_left, "x", LEFT))
    take_sum = lax.ppermute(give_sum, "core", SWAP)
    weight_grad = weight_sum(
        acts, places, grad_late.reshape(16, 4, sub, cols), core, (take_sum,), float(32 * tok) ** (-0.5)
    )
    term_right, term_left, weight_grad = tie(term_right, term_left, weight_grad)

    slope = gelu_slope(rows.reshape(4 * tok, ff).astype(f32))
    from_left = jnp.concatenate([sum_right, term_right]).astype(f32)
    from_right = jnp.concatenate([term_left, sum_left]).astype(f32)
    summed = home.reshape(4 * tok, ff).astype(f32) + from_left + from_right
    (grad_here,) = tie((summed * slope).astype(bf16).reshape(4, 1, tok, ff))
    keep = lax.dynamic_slice(grad_here, (0, 0, 0, ff_dev * core), (4, 1, tok, ff_dev))
    give = lax.dynamic_slice(grad_here, (0, 0, 0, ff_dev * (1 - core)), (4, 1, tok, ff_dev))
    take = lax.ppermute(give, "core", SWAP)
    hidden_grad = jnp.zeros((4, 2, tok, ff_dev), bf16)
    hidden_grad = lax.dynamic_update_slice(hidden_grad, keep, (0, core, 0, 0))
    hidden_grad = lax.dynamic_update_slice(hidden_grad, take, (0, 1 - core, 0, 0))
    hidden_grad = hidden_grad.reshape(8 * tok, ff_dev)

    ffn_out = jnp.zeros((4, sub, cols), bf16)
    for terms, ends in ((terms_a, places[:2]), (terms_b, places[2:])):
        done = jnp.sum(terms.astype(f32), axis=0).astype(bf16)
        for which, j in enumerate(ends):
            ffn_out = lax.dynamic_update_slice(ffn_out, done[which][None], (j, 0, 0))
    return (ffn_out.reshape(tok, cols), hidden_grad, weight_grad)


def solution(mesh):
    fine = Mesh(mesh.devices.reshape(4, 4, 2, 4), ("y", "z", "core", "x"))
    row = ("y", "z", "core")
    return jax.shard_map(
        body,
        mesh=fine,
        in_specs=(P(row, None), P(row, "x"), P(row, "x")),
        out_specs=(P(row, "x"), P("x", row), P(row, "x")),
        check_vma=False,
    )
```

profile of v0, /device:TPU:1, one launch (start us, length us, event | category | flops | bytes accessed | tf_op | source)
XLA Modules:
  0.0 227.6 jit_solution(17323032624711027000)
XLA Ops:
  0.6 3.6 %split_quarter.1 = bf16[16,32,1536]{2,1,0:T(8,128)(2,1)} custom-call(s32[1]{0:T(128)} %bitcast.x_ref, bf16[128,24576]{1,0:T(8,128)(2,1)} %rows_ref.1), custom_call_target="tpu_custom_call" | custom-call | tf_op jit(solution)/shard_map/split_quarter/pallas_call | solution.py:74
  4.3 2.5 %collective-permute-start.2 = (bf16[128,1536]{1,0:T(8,128)(2,1)S(1)}, bf16[128,1536]{1,0:T(8,128)(2,1)S(1)}, u32[]{:S(2)}, u32[]{:S(2)}) collective-permute-start(bf16[128,1536]{1,0:T(8,128)(2,1)S(1)} %copy-done.12), channel_id=1, source_target_pairs={{0,8},{8,16},{16,24},{24,0},{1,9},{9,17},{17,25},{25,1},{2,10},{10... | collective-permute-start | bytes 1179656 | tf_op jit(solution)/shard_map/ppermute | solution.py:38
  8.9 5.5 %all-to-all-start = ((bf16[16,32,1536]{2,1,0:T(8,128)(2,1)}), bf16[16,32,1536]{2,1,0:T(8,128)(2,1)S(1)}, u32[]{:S(2)}, u32[]{:S(2)}) async-start(bf16[16,32,1536]{2,1,0:T(8,128)(2,1)} %split_quarter.1), calls=%async_computation | async-start | bytes 3145728 | tf_op jit(solution)/shard_map/all_to_all | solution.py:160
  22.5 16.6 %collective-permute-done.4 = bf16[64,1536]{1,0:T(8,128)(2,1)S(1)} collective-permute-done((bf16[64,1536]{1,0:T(8,128)(2,1)S(1)}, bf16[64,1536]{1,0:T(8,128)(2,1)S(1)}, u32[]{:S(2)}, u32[]{:S(2)}) %collective-permute-start.4) | collective-permute-done | bytes 196640 | tf_op jit(solution)/shard_map/ppermute | solution.py:43
  48.5 4.0 %maximum_select_fusion = bf16[1536,1536]{1,0:T(8,128)(2,1)S(1)} fusion(bf16[768,1536]{1,0:T(8,128)(2,1)} %collective-permute-done.6, bf16[768,1536]{1,0:T(8,128)(2,1)S(1)} %copy-done.5, pred[]{:T(512)S(6)} %eq.3), kind=kLoop, calls=%fused_computation.27 | loop fusion | flops 21233664 | bytes 9437185 | tf_op jit(solution)/shard_map/jit(_where)/select_n | solution.py:194
  52.5 2.6 %convolution_convert_fusion.7 = bf16[512,1536]{1,0:T(8,128)(2,1)S(1)} fusion(bf16[512,1536]{1,0:T(8,128)(2,1)S(1)} %bitcast.115, bf16[1536,1536]{1,0:T(8,128)(2,1)S(1)} %maximum_select_fusion), kind=kOutput, calls=%fused_computation.68 | convolution fusion | flops 2416705536 | bytes 7864320 | tf_op jit(solution)/shard_map/dot_general | solution.py:174
  55.1 3.3 %broadcast_in_dim.61 = bf16[4,4,128,1536]{3,2,1,0:T(8,128)(2,1)} broadcast(bf16[]{:T(256)} %constant.81.clone.1), dimensions={} | broadcast | bytes 6291458 | tf_op jit(solution)/shard_map/broadcast_in_dim | solution.py:49
  58.4 2.7 %bitcast_dynamic-update-slice_fusion.2 = bf16[4,4,128,1536]{3,2,1,0:T(8,128)(2,1)} fusion(bf16[4,4,128,1536]{3,2,1,0:T(8,128)(2,1)} %broadcast_in_dim.61, s32[]{:T(128)S(6)} %select_n.82, bf16[4,128,1536]{2,1,0:T(8,128)(2,1)} %fusion.32), kind=kLoop, calls=%fused_computation.79 | loop fusion | bytes 3145732 | tf_op jit(solution)/shard_map/dynamic_update_slice | solution.py:53
  61.1 15.0 %collective-permute-done = bf16[4,4,32,1536]{3,2,1,0:T(8,128)(2,1)S(1)} collective-permute-done((bf16[4,4,32,1536]{3,2,1,0:T(8,128)(2,1)S(1)}, bf16[4,4,32,1536]{3,2,1,0:T(8,128)(2,1)S(1)}, u32[]{:S(2)}, u32[]{:S(2)}) %collective-permute-start) | collective-permute-done | bytes 1572896 | tf_op jit(solution)/shard_map/ppermute | solution.py:38
  76.1 4.6 %collective-permute-done.7 = bf16[4,128,1536]{2,1,0:T(8,128)(2,1)S(1)} collective-permute-done((bf16[4,128,1536]{2,1,0:T(8,128)(2,1)}, bf16[4,128,1536]{2,1,0:T(8,128)(2,1)S(1)}, u32[]{:S(2)}, u32[]{:S(2)}) %collective-permute-start.7) | collective-permute-done | bytes 1572896 | tf_op jit(solution)/shard_map/ppermute | solution.py:38
  83.1 2.7 %collective-permute-start.10 = (bf16[2,4,32,1536]{3,2,1,0:T(8,128)(2,1)S(1)}, bf16[2,4,32,1536]{3,2,1,0:T(8,128)(2,1)}, u32[]{:S(2)}, u32[]{:S(2)}) collective-permute-start(bf16[2,4,32,1536]{3,2,1,0:T(8,128)(2,1)S(1)} %slice.51), channel_id=1, source_target_pairs={{0,3},{1,0},{2,1},{3,2},{4,7},{5,4},{6,5},{7,6},{8,11},{9,8},{10,9... | collective-permute-start | bytes 2359304 | tf_op jit(solution)/shard_map/ppermute | solution.py:43
  88.9 2.6 %convolution_convert_fusion.6 = bf16[512,1536]{1,0:T(8,128)(2,1)S(1)} fusion(bf16[512,1536]{1,0:T(8,128)(2,1)S(1)} %bitcast.118, bf16[1536,1536]{1,0:T(8,128)(2,1)S(1)} %maximum_select_fusion), kind=kOutput, calls=%fused_computation.67 | convolution fusion | flops 2416705536 | bytes 7864320 | tf_op jit(solution)/shard_map/dot_general | solution.py:174
  91.5 3.7 %convolution_convert_fusion.5 = bf16[512,1536]{1,0:T(8,128)(2,1)} fusion(bf16[512,1536]{1,0:T(8,128)(2,1)S(1)} %bitcast.121, bf16[1536,1536]{1,0:T(8,128)(2,1)S(1)} %maximum_select_fusion), kind=kOutput, calls=%fused_computation.66 | convolution fusion | flops 2416705536 | bytes 7864320 | tf_op jit(solution)/shard_map/dot_general | solution.py:174
  104.2 7.6 %all-to-all-start.1 = ((bf16[16,2,32,1536]{3,2,1,0:T(8,128)(2,1)}), bf16[16,2,32,1536]{3,2,1,0:T(8,128)(2,1)}, u32[]{:S(2)}, u32[]{:S(2)}) async-start(bf16[16,2,32,1536]{3,2,1,0:T(8,128)(2,1)} %pad_maximum_fusion), calls=%async_computation.1 | async-start | bytes 6291456 | tf_op jit(solution)/shard_map/all_to_all | solution.py:185
  111.7 2.6 %fusion.29 = bf16[4,4,128,1536]{3,2,1,0:T(8,128)(2,1)} fusion(bf16[4,4,128,1536]{3,2,1,0:T(8,128)(2,1)} %bitcast_dynamic-update-slice_fusion, s32[]{:T(128)S(6)} %select_n.85, bf16[2,128,1536]{2,1,0:T(8,128)(2,1)} %copy-done.11, bf16[2,128,1536]{2,1,0:T(8,128)(2,1)} %copy-done.10), kind=kLoop, calls=%fused_computation.70 | loop fusion | flops 3145728 | bytes 3145732 | tf_op jit(solution)/shard_map/dynamic_update_slice | solution.py:53
  116.0 5.1 %convolution_convert_fusion.4 = bf16[512,1536]{1,0:T(8,128)(2,1)S(1)} fusion(bf16[512,1536]{1,0:T(8,128)(2,1)S(1)} %bitcast.146, bf16[1536,1536]{1,0:T(8,128)(2,1)} %copy-done.4), kind=kOutput, calls=%fused_computation.65 | convolution fusion | flops 2416705536 | bytes 7864320 | tf_op jit(solution)/shard_map/dot_general | solution.py:180
  121.3 2.7 %collective-permute-start.14 = (bf16[256,1536]{1,0:T(8,128)(2,1)S(1)}, bf16[256,1536]{1,0:T(8,128)(2,1)S(1)}, u32[]{:S(2)}, u32[]{:S(2)}) collective-permute-start(bf16[256,1536]{1,0:T(8,128)(2,1)S(1)} %get-tuple-element.133), channel_id=1, source_target_pairs={{0,3},{1,0},{2,1},{3,2},{4,7},{5,4},{6,5},{7,6},{8,11},{9,8},{10,9... | collective-permute-start | bytes 2359304 | tf_op jit(solution)/shard_map/ppermute | solution.py:222
  126.1 2.6 %convolution_convert_fusion.3 = bf16[512,1536]{1,0:T(8,128)(2,1)S(1)} fusion(bf16[512,1536]{1,0:T(8,128)(2,1)S(1)} %bitcast.149, bf16[1536,1536]{1,0:T(8,128)(2,1)S(1)} %bitcast.134), kind=kOutput, calls=%fused_computation.64 | convolution fusion | flops 2416705536 | bytes 7864320 | tf_op jit(solution)/shard_map/dot_general | solution.py:180
  128.7 2.6 %convolution_convert_fusion.2 = bf16[512,1536]{1,0:T(8,128)(2,1)S(1)} fusion(bf16[512,1536]{1,0:T(8,128)(2,1)S(1)} %bitcast.148, bf16[1536,1536]{1,0:T(8,128)(2,1)S(1)} %bitcast.134), kind=kOutput, calls=%fused_computation.63 | convolution fusion | flops 2416705536 | bytes 7864320 | tf_op jit(solution)/shard_map/dot_general | solution.py:180
  135.5 2.6 %convolution_convert_fusion.1 = bf16[512,1536]{1,0:T(8,128)(2,1)S(1)} fusion(bf16[512,1536]{1,0:T(8,128)(2,1)S(1)} %bitcast.124, bf16[1536,1536]{1,0:T(8,128)(2,1)S(1)} %bitcast.134), kind=kOutput, calls=%fused_computation.62 | convolution fusion | flops 2416705536 | bytes 7864320 | tf_op jit(solution)/shard_map/dot_general | solution.py:174
  143.1 2.7 %collective-permute-start.16 = (bf16[256,1536]{1,0:T(8,128)(2,1)}, bf16[256,1536]{1,0:T(8,128)(2,1)}, u32[]{:S(2)}, u32[]{:S(2)}) collective-permute-start(bf16[256,1536]{1,0:T(8,128)(2,1)} %fusion.30), channel_id=1, source_target_pairs={{0,3},{1,0},{2,1},{3,2},{4,7},{5,4},{6,5},{7,6},{8,11},{9,8},{10,9... | collective-permute-start | bytes 2359304 | tf_op jit(solution)/shard_map/ppermute | solution.py:233
  147.3 3.7 %convolution_convert_fusion = bf16[512,1536]{1,0:T(8,128)(2,1)} fusion(bf16[512,1536]{1,0:T(8,128)(2,1)S(1)} %bitcast.145, bf16[1536,1536]{1,0:T(8,128)(2,1)S(1)} %bitcast.134), kind=kOutput, calls=%fused_computation.61 | convolution fusion | flops 2416705536 | bytes 7864320 | tf_op jit(solution)/shard_map/dot_general | solution.py:180
  152.0 6.7 %all-to-all-start.2 = ((bf16[16,2,32,1536]{3,2,1,0:T(8,128)(2,1)}), bf16[16,2,32,1536]{3,2,1,0:T(8,128)(2,1)}, u32[]{:S(2)}, u32[]{:S(2)}) async-start(bf16[16,2,32,1536]{3,2,1,0:T(8,128)(2,1)} %pad_maximum_fusion.1), calls=%async_computation.2 | async-start | bytes 6291456 | tf_op jit(solution)/shard_map/all_to_all | solution.py:185
  162.4 10.3 %weight_sum.2 = bf16[768,1536]{1,0:T(8,128)(2,1)} custom-call(s32[5]{0:T(128)S(1)} %stack.33.at_ref, bf16[512,1536]{1,0:T(8,128)(2,1)S(1)} %bitcast.116, bf16[512,1536]{1,0:T(8,128)(2,1)S(1)} %bitcast.119, bf16[512,1536]{1,0:T(8,128)(2,1)S(1)} %bitcast.122, bf16[512,1536]{1,0:T(8,128)(2,1)} %bitcast.125, bf16[16,4,32,1536]{3,2,1,0:T(8,128)(2,1)} %bitcast.50.grad_0.grad_1, ...), custom_call_target="tpu_custom_call" | custom-call | flops 4831838208 | bytes 14155776 | tf_op jit(solution)/shard_map/weight_sum/pallas_call | solution.py:127
  172.7 6.0 %collective-permute-start.19 = (bf16[768,1536]{1,0:T(8,128)(2,1)}, bf16[768,1536]{1,0:T(8,128)(2,1)}, u32[]{:S(2)}, u32[]{:S(2)}) collective-permute-start(bf16[768,1536]{1,0:T(8,128)(2,1)} %weight_sum.2), channel_id=1, source_target_pairs={{0,4},{4,0},{1,5},{5,1},{2,6},{6,2},{3,7},{7,3},{8,12},{12,8},{9,1... | collective-permute-start | bytes 7077896 | tf_op jit(solution)/shard_map/ppermute | solution.py:244
  178.7 2.3 %reduce_sum.24 = bf16[2,32,1536]{2,1,0:T(8,128)(2,1)S(1)} reduce(bf16[16,2,32,1536]{3,2,1,0:T(8,128)(2,1)} %all-to-all-done.1, bf16[]{:T(256)} %constant.81.clone.1), dimensions={0}, to_apply=%region_0.1 | reduce | flops 1474560 | bytes 3342338 | tf_op jit(solution)/shard_map/reduce_sum | solution.py:265
  181.2 2.7 %collective-permute-start.18 = (bf16[256,1536]{1,0:T(8,128)(2,1)}, bf16[256,1536]{1,0:T(8,128)(2,1)}, u32[]{:S(2)}, u32[]{:S(2)}) collective-permute-start(bf16[256,1536]{1,0:T(8,128)(2,1)} %slice_bitcast_fusion), channel_id=1, source_target_pairs={{0,3},{1,0},{2,1},{3,2},{4,7},{5,4},{6,5},{7,6},{8,11},{9,8},{10,9... | collective-permute-start | bytes 2359304 | tf_op jit(solution)/shard_map/ppermute | solution.py:243
  185.9 7.9 %all-to-all-done.2 = bf16[16,2,32,1536]{3,2,1,0:T(8,128)(2,1)} async-done(((bf16[16,2,32,1536]{3,2,1,0:T(8,128)(2,1)}), bf16[16,2,32,1536]{3,2,1,0:T(8,128)(2,1)}, u32[]{:S(2)}, u32[]{:S(2)}) %all-to-all-start.2) | async-done | bytes 3145760 | tf_op jit(solution)/shard_map/all_to_all | solution.py:185
  196.1 5.7 %collective-permute-done.17 = bf16[256,1536]{1,0:T(8,128)(2,1)} collective-permute-done((bf16[256,1536]{1,0:T(8,128)(2,1)}, bf16[256,1536]{1,0:T(8,128)(2,1)}, u32[]{:S(2)}, u32[]{:S(2)}) %collective-permute-start.17) | collective-permute-done | bytes 786464 | tf_op jit(solution)/shard_map/ppermute | solution.py:243
  203.3 11.3 %weight_sum.3 = bf16[768,1536]{1,0:T(8,128)(2,1)} custom-call(s32[5]{0:T(128)S(1)} %stack.35.at_ref, bf16[512,1536]{1,0:T(8,128)(2,1)S(1)} %bitcast.117, bf16[512,1536]{1,0:T(8,128)(2,1)S(1)} %bitcast.120, bf16[512,1536]{1,0:T(8,128)(2,1)S(1)} %bitcast.123, bf16[512,1536]{1,0:T(8,128)(2,1)} %bitcast.126, bf16[16,4,32,1536]{3,2,1,0:T(8,128)(2,1)} %bitcast.54.grad_0.grad_1, ...), custom_call_target="tpu_custom_call" | custom-call | flops 4831838208 | bytes 14155776 | tf_op jit(solution)/shard_map/weight_sum/pallas_call | solution.py:127
  217.6 3.8 %fusion.27 = bf16[4,1,128,1536]{3,2,1,0:T(8,128)(2,1)S(1)} fusion(bf16[4,1,128,1536]{3,2,1,0:T(8,128)(2,1)S(1)} %bitcast.131, bf16[4,1,128,1536]{3,2,1,0:T(8,128)(2,1)S(1)} %bitcast.132, bf16[4,1,128,1536]{3,2,1,0:T(8,128)(2,1)S(1)} %bitcast.147, bf16[4,1,128,1536]{3,2,1,0:T(8,128)(2,1)} %bitcast.114), kind=kLoop, calls=%fused_computation.55 | loop fusion | flops 19660800 | bytes 7864320 | tf_op jit(solution)/shard_map/convert_element_type | solution.py:254
  221.7 2.9 %collective-permute-start.20 = (bf16[4,1,128,768]{3,2,1,0:T(8,128)(2,1)S(1)}, bf16[4,1,128,768]{3,2,1,0:T(8,128)(2,1)S(1)}, u32[]{:S(2)}, u32[]{:S(2)}) collective-permute-start(bf16[4,1,128,768]{3,2,1,0:T(8,128)(2,1)S(1)} %get-tuple-element.131), channel_id=1, source_target_pairs={{0,4},{4,0},{1,5},{5,1},{2,6},{6,2},{3,7},{7,3},{8,12},{12,8},{9,1... | collective-permute-start | bytes 2359304 | tf_op jit(solution)/shard_map/ppermute | solution.py:257
  (110 shorter events, 65.6 us)
Async XLA Ops:
  0.6 3.6 %copy-start.12 = (bf16[128,1536]{1,0:T(8,128)(2,1)S(1)}, bf16[128,1536]{1,0:T(8,128)(2,1)}, u32[]{:S(2)}) copy-start(bf16[128,1536]{1,0:T(8,128)(2,1)} %param.5) | copy-start | bytes 1179652
  4.3 13.7 %collective-permute-start.2 = (bf16[128,1536]{1,0:T(8,128)(2,1)S(1)}, bf16[128,1536]{1,0:T(8,128)(2,1)S(1)}, u32[]{:S(2)}, u32[]{:S(2)}) collective-permute-start(bf16[128,1536]{1,0:T(8,128)(2,1)S(1)} %copy-done.12), channel_id=1, source_target_pairs={{0,8},{8,16},{16,24},{24,0},{1,9},{9,17},{17,25},{25,1},{2,10},{10... | collective-permute-start | bytes 1179656 | tf_op jit(solution)/shard_map/ppermute | solution.py:38
  6.7 11.2 %collective-permute-start.3 = (bf16[128,1536]{1,0:T(8,128)(2,1)S(1)}, bf16[128,1536]{1,0:T(8,128)(2,1)S(1)}, u32[]{:S(2)}, u32[]{:S(2)}) collective-permute-start(bf16[128,1536]{1,0:T(8,128)(2,1)S(1)} %copy-done.12), channel_id=1, source_target_pairs={{0,24},{8,0},{16,8},{24,16},{1,25},{9,1},{17,9},{25,17},{2,26},{10... | collective-permute-start | bytes 1179656 | tf_op jit(solution)/shard_map/ppermute | solution.py:38
  8.9 31.0 %all-to-all-start = ((bf16[16,32,1536]{2,1,0:T(8,128)(2,1)}), bf16[16,32,1536]{2,1,0:T(8,128)(2,1)S(1)}, u32[]{:S(2)}, u32[]{:S(2)}) async-start(bf16[16,32,1536]{2,1,0:T(8,128)(2,1)} %split_quarter.1), calls=%async_computation | async-start | bytes 3145728 | tf_op jit(solution)/shard_map/all_to_all | solution.py:160
  14.3 31.4 %collective-permute-start.6 = (bf16[768,1536]{1,0:T(8,128)(2,1)}, bf16[768,1536]{1,0:T(8,128)(2,1)}, u32[]{:S(2)}, u32[]{:S(2)}) collective-permute-start(bf16[768,1536]{1,0:T(8,128)(2,1)} %param.4), channel_id=1, source_target_pairs={{0,4},{4,0},{1,5},{5,1},{2,6},{6,2},{3,7},{7,3},{8,12},{12,8},{9,1... | collective-permute-start | bytes 7077896 | tf_op jit(solution)/shard_map/ppermute | solution.py:166
  18.0 21.1 %collective-permute-start.4 = (bf16[64,1536]{1,0:T(8,128)(2,1)S(1)}, bf16[64,1536]{1,0:T(8,128)(2,1)S(1)}, u32[]{:S(2)}, u32[]{:S(2)}) collective-permute-start(bf16[64,1536]{1,0:T(8,128)(2,1)S(1)} %slice.48), channel_id=1, source_target_pairs={{0,8},{8,16},{16,24},{24,0},{1,9},{9,17},{17,25},{25,1},{2,10},{10... | collective-permute-start | bytes 589832 | tf_op jit(solution)/shard_map/ppermute | solution.py:43
  19.7 19.4 %collective-permute-start.5 = (bf16[64,1536]{1,0:T(8,128)(2,1)S(1)}, bf16[64,1536]{1,0:T(8,128)(2,1)S(1)}, u32[]{:S(2)}, u32[]{:S(2)}) collective-permute-start(bf16[64,1536]{1,0:T(8,128)(2,1)S(1)} %slice.49), channel_id=1, source_target_pairs={{0,24},{8,0},{16,8},{24,16},{1,25},{9,1},{17,9},{25,17},{2,26},{10... | collective-permute-start | bytes 589832 | tf_op jit(solution)/shard_map/ppermute | solution.py:43
  39.9 8.6 %copy-start.5 = (bf16[768,1536]{1,0:T(8,128)(2,1)S(1)}, bf16[768,1536]{1,0:T(8,128)(2,1)}, u32[]{:S(2)}) copy-start(bf16[768,1536]{1,0:T(8,128)(2,1)} %param.4) | copy-start | bytes 7077892
  39.9 36.2 %collective-permute-start = (bf16[4,4,32,1536]{3,2,1,0:T(8,128)(2,1)S(1)}, bf16[4,4,32,1536]{3,2,1,0:T(8,128)(2,1)S(1)}, u32[]{:S(2)}, u32[]{:S(2)}) collective-permute-start(bf16[4,4,32,1536]{3,2,1,0:T(8,128)(2,1)S(1)} %bitcast.127), channel_id=1, source_target_pairs={{0,1},{1,2},{2,3},{3,0},{4,5},{5,6},{6,7},{7,4},{8,9},{9,10},{10,1... | collective-permute-start | bytes 4718600 | tf_op jit(solution)/shard_map/ppermute | solution.py:38
  41.1 35.0 %collective-permute-start.1 = (bf16[4,4,32,1536]{3,2,1,0:T(8,128)(2,1)S(1)}, bf16[4,4,32,1536]{3,2,1,0:T(8,128)(2,1)S(1)}, u32[]{:S(2)}, u32[]{:S(2)}) collective-permute-start(bf16[4,4,32,1536]{3,2,1,0:T(8,128)(2,1)S(1)} %bitcast.128), channel_id=1, source_target_pairs={{0,3},{1,0},{2,1},{3,2},{4,7},{5,4},{6,5},{7,6},{8,11},{9,8},{10,9... | collective-permute-start | bytes 4718600 | tf_op jit(solution)/shard_map/ppermute | solution.py:38
  45.8 34.9 %collective-permute-start.7 = (bf16[4,128,1536]{2,1,0:T(8,128)(2,1)}, bf16[4,128,1536]{2,1,0:T(8,128)(2,1)S(1)}, u32[]{:S(2)}, u32[]{:S(2)}) collective-permute-start(bf16[4,128,1536]{2,1,0:T(8,128)(2,1)} %fusion.32), channel_id=1, source_target_pairs={{0,32},{32,64},{64,96},{96,0},{1,33},{33,65},{65,97},{97,1},{2,34}... | collective-permute-start | bytes 4718600 | tf_op jit(solution)/shard_map/ppermute | solution.py:38
  47.0 33.8 %collective-permute-start.8 = (bf16[4,128,1536]{2,1,0:T(8,128)(2,1)}, bf16[4,128,1536]{2,1,0:T(8,128)(2,1)S(1)}, u32[]{:S(2)}, u32[]{:S(2)}) collective-permute-start(bf16[4,128,1536]{2,1,0:T(8,128)(2,1)} %fusion.32), channel_id=1, source_target_pairs={{0,96},{32,0},{64,32},{96,64},{1,97},{33,1},{65,33},{97,65},{2,98}... | collective-permute-start | bytes 4718600 | tf_op jit(solution)/shard_map/ppermute | solution.py:38
  52.5 39.0 %copy-start.4 = (bf16[1536,1536]{1,0:T(8,128)(2,1)}, bf16[1536,1536]{1,0:T(8,128)(2,1)S(1)}, u32[]{:S(2)}) copy-start(bf16[1536,1536]{1,0:T(8,128)(2,1)S(1)} %maximum_select_fusion) | copy-start | bytes 14155780
  83.0 8.5 %copy-start = (bf16[4,4,32,1536]{3,2,1,0:T(8,128)(2,1)}, bf16[4,4,32,1536]{3,2,1,0:T(8,128)(2,1)S(1)}, u32[]{:S(2)}) copy-start(bf16[4,4,32,1536]{3,2,1,0:T(8,128)(2,1)S(1)} %get-tuple-element.114) | copy-start | bytes 4718596
  83.1 18.3 %collective-permute-start.9 = (bf16[2,4,32,1536]{3,2,1,0:T(8,128)(2,1)S(1)}, bf16[2,4,32,1536]{3,2,1,0:T(8,128)(2,1)}, u32[]{:S(2)}, u32[]{:S(2)}) collective-permute-start(bf16[2,4,32,1536]{3,2,1,0:T(8,128)(2,1)S(1)} %slice.50), channel_id=1, source_target_pairs={{0,1},{1,2},{2,3},{3,0},{4,5},{5,6},{6,7},{7,4},{8,9},{9,10},{10,1... | collective-permute-start | bytes 2359304 | tf_op jit(solution)/shard_map/ppermute | solution.py:43
  83.1 18.2 %collective-permute-start.10 = (bf16[2,4,32,1536]{3,2,1,0:T(8,128)(2,1)S(1)}, bf16[2,4,32,1536]{3,2,1,0:T(8,128)(2,1)}, u32[]{:S(2)}, u32[]{:S(2)}) collective-permute-start(bf16[2,4,32,1536]{3,2,1,0:T(8,128)(2,1)S(1)} %slice.51), channel_id=1, source_target_pairs={{0,3},{1,0},{2,1},{3,2},{4,7},{5,4},{6,5},{7,6},{8,11},{9,8},{10,9... | collective-permute-start | bytes 2359304 | tf_op jit(solution)/shard_map/ppermute | solution.py:43
  85.9 16.5 %collective-permute-start.11 = (bf16[2,128,1536]{2,1,0:T(8,128)(2,1)S(1)}, bf16[2,128,1536]{2,1,0:T(8,128)(2,1)S(1)}, u32[]{:S(2)}, u32[]{:S(2)}) collective-permute-start(bf16[2,128,1536]{2,1,0:T(8,128)(2,1)S(1)} %slice.52), channel_id=1, source_target_pairs={{0,32},{32,64},{64,96},{96,0},{1,33},{33,65},{65,97},{97,1},{2,34}... | collective-permute-start | bytes 2359304 | tf_op jit(solution)/shard_map/ppermute | solution.py:43
  87.5 15.4 %collective-permute-start.12 = (bf16[2,128,1536]{2,1,0:T(8,128)(2,1)S(1)}, bf16[2,128,1536]{2,1,0:T(8,128)(2,1)S(1)}, u32[]{:S(2)}, u32[]{:S(2)}) collective-permute-start(bf16[2,128,1536]{2,1,0:T(8,128)(2,1)S(1)} %slice.53), channel_id=1, source_target_pairs={{0,96},{32,0},{64,32},{96,64},{1,97},{33,1},{65,33},{97,65},{2,98}... | collective-permute-start | bytes 2359304 | tf_op jit(solution)/shard_map/ppermute | solution.py:43
  104.2 47.9 %all-to-all-start.1 = ((bf16[16,2,32,1536]{3,2,1,0:T(8,128)(2,1)}), bf16[16,2,32,1536]{3,2,1,0:T(8,128)(2,1)}, u32[]{:S(2)}, u32[]{:S(2)}) async-start(bf16[16,2,32,1536]{3,2,1,0:T(8,128)(2,1)} %pad_maximum_fusion), calls=%async_computation.1 | async-start | bytes 6291456 | tf_op jit(solution)/shard_map/all_to_all | solution.py:185
  114.4 11.7 %slice-start = ((s8[4718592]{0:T(1024)(128)(4,1)}), s8[4194304]{0:T(1024)(128)(4,1)S(1)}, s32[]{:S(2)}) async-start(s8[4718592]{0:T(1024)(128)(4,1)} %bitcast.133), calls=%async_computation.3 | async-start | bytes 8388608
  116.0 10.1 %slice-start.1 = ((s8[4718592]{0:T(1024)(128)(4,1)}), s8[524288]{0:T(1024)(128)(4,1)S(1)}, s32[]{:S(2)}) async-start(s8[4718592]{0:T(1024)(128)(4,1)} %bitcast.133), calls=%async_computation.4 | async-start | bytes 1048576
  121.2 19.6 %collective-permute-start.13 = (bf16[256,1536]{1,0:T(8,128)(2,1)S(1)}, bf16[256,1536]{1,0:T(8,128)(2,1)S(1)}, u32[]{:S(2)}, u32[]{:S(2)}) collective-permute-start(bf16[256,1536]{1,0:T(8,128)(2,1)S(1)} %get-tuple-element.134), channel_id=1, source_target_pairs={{0,1},{1,2},{2,3},{3,0},{4,5},{5,6},{6,7},{7,4},{8,9},{9,10},{10,1... | collective-permute-start | bytes 2359304 | tf_op jit(solution)/shard_map/ppermute | solution.py:222
  121.3 19.6 %collective-permute-start.14 = (bf16[256,1536]{1,0:T(8,128)(2,1)S(1)}, bf16[256,1536]{1,0:T(8,128)(2,1)S(1)}, u32[]{:S(2)}, u32[]{:S(2)}) collective-permute-start(bf16[256,1536]{1,0:T(8,128)(2,1)S(1)} %get-tuple-element.133), channel_id=1, source_target_pairs={{0,3},{1,0},{2,1},{3,2},{4,7},{5,4},{6,5},{7,6},{8,11},{9,8},{10,9... | collective-permute-start | bytes 2359304 | tf_op jit(solution)/shard_map/ppermute | solution.py:222
  131.4 10.7 %copy-start.7 = (bf16[512,1536]{1,0:T(8,128)(2,1)}, bf16[512,1536]{1,0:T(8,128)(2,1)S(1)}, u32[]{:S(2)}) copy-start(bf16[512,1536]{1,0:T(8,128)(2,1)S(1)} %convolution_convert_fusion.2) | copy-start | bytes 4718596
  135.4 3.4 %copy-start.8 = (bf16[512,1536]{1,0:T(8,128)(2,1)S(1)}, bf16[512,1536]{1,0:T(8,128)(2,1)}, u32[]{:S(2)}) copy-start(bf16[512,1536]{1,0:T(8,128)(2,1)} %convolution_convert_fusion.5) | copy-start | bytes 4718596
  142.0 18.9 %collective-permute-start.15 = (bf16[256,1536]{1,0:T(8,128)(2,1)}, bf16[256,1536]{1,0:T(8,128)(2,1)}, u32[]{:S(2)}, u32[]{:S(2)}) collective-permute-start(bf16[256,1536]{1,0:T(8,128)(2,1)} %fusion.31), channel_id=1, source_target_pairs={{0,1},{1,2},{2,3},{3,0},{4,5},{5,6},{6,7},{7,4},{8,9},{9,10},{10,1... | collective-permute-start | bytes 2359304 | tf_op jit(solution)/shard_map/ppermute | solution.py:233
  143.1 17.8 %collective-permute-start.16 = (bf16[256,1536]{1,0:T(8,128)(2,1)}, bf16[256,1536]{1,0:T(8,128)(2,1)}, u32[]{:S(2)}, u32[]{:S(2)}) collective-permute-start(bf16[256,1536]{1,0:T(8,128)(2,1)} %fusion.30), channel_id=1, source_target_pairs={{0,3},{1,0},{2,1},{3,2},{4,7},{5,4},{6,5},{7,6},{8,11},{9,8},{10,9... | collective-permute-start | bytes 2359304 | tf_op jit(solution)/shard_map/ppermute | solution.py:233
  152.0 41.7 %all-to-all-start.2 = ((bf16[16,2,32,1536]{3,2,1,0:T(8,128)(2,1)}), bf16[16,2,32,1536]{3,2,1,0:T(8,128)(2,1)}, u32[]{:S(2)}, u32[]{:S(2)}) async-start(bf16[16,2,32,1536]{3,2,1,0:T(8,128)(2,1)} %pad_maximum_fusion.1), calls=%async_computation.2 | async-start | bytes 6291456 | tf_op jit(solution)/shard_map/all_to_all | solution.py:185
  172.7 29.2 %collective-permute-start.19 = (bf16[768,1536]{1,0:T(8,128)(2,1)}, bf16[768,1536]{1,0:T(8,128)(2,1)}, u32[]{:S(2)}, u32[]{:S(2)}) collective-permute-start(bf16[768,1536]{1,0:T(8,128)(2,1)} %weight_sum.2), channel_id=1, source_target_pairs={{0,4},{4,0},{1,5},{5,1},{2,6},{6,2},{3,7},{7,3},{8,12},{12,8},{9,1... | collective-permute-start | bytes 7077896 | tf_op jit(solution)/shard_map/ppermute | solution.py:244
  181.1 20.8 %collective-permute-start.17 = (bf16[256,1536]{1,0:T(8,128)(2,1)}, bf16[256,1536]{1,0:T(8,128)(2,1)}, u32[]{:S(2)}, u32[]{:S(2)}) collective-permute-start(bf16[256,1536]{1,0:T(8,128)(2,1)} %slice_bitcast_fusion.1), channel_id=1, source_target_pairs={{0,1},{1,2},{2,3},{3,0},{4,5},{5,6},{6,7},{7,4},{8,9},{9,10},{10,1... | collective-permute-start | bytes 2359304 | tf_op jit(solution)/shard_map/ppermute | solution.py:243
  181.2 20.7 %collective-permute-start.18 = (bf16[256,1536]{1,0:T(8,128)(2,1)}, bf16[256,1536]{1,0:T(8,128)(2,1)}, u32[]{:S(2)}, u32[]{:S(2)}) collective-permute-start(bf16[256,1536]{1,0:T(8,128)(2,1)} %slice_bitcast_fusion), channel_id=1, source_target_pairs={{0,3},{1,0},{2,1},{3,2},{4,7},{5,4},{6,5},{7,6},{8,11},{9,8},{10,9... | collective-permute-start | bytes 2359304 | tf_op jit(solution)/shard_map/ppermute | solution.py:243
  221.7 4.8 %collective-permute-start.20 = (bf16[4,1,128,768]{3,2,1,0:T(8,128)(2,1)S(1)}, bf16[4,1,128,768]{3,2,1,0:T(8,128)(2,1)S(1)}, u32[]{:S(2)}, u32[]{:S(2)}) collective-permute-start(bf16[4,1,128,768]{3,2,1,0:T(8,128)(2,1)S(1)} %get-tuple-element.131), channel_id=1, source_target_pairs={{0,4},{4,0},{1,5},{5,1},{2,6},{6,2},{3,7},{7,3},{8,12},{12,8},{9,1... | collective-permute-start | bytes 2359304 | tf_op jit(solution)/shard_map/ppermute | solution.py:257
  (7 other events, 11.5 us)
where the time goes:
time: 228 us
  starting transfers between devices  56.9 us (25%)
  waiting for transfers between devices  52 us (23%)
  local copies, waits for them, and re-layouts  37.5 us (16%)
  other arithmetic  29.3 us (13%)
  matrix products  25.6 us (11%)
  Pallas kernels  25.2 us (11%)
    pallas_call x2, Pallas kernels, weight_sum(): pl.pallas_call(functools.partial(weight_kernel, scale), grid_spec=pltpu.P...  21.6 us
    ppermute x3, waiting for transfers between devices, shift(): lax.ppermute(block, axis, RIGHT)  19.6 us
    ppermute x3, waiting for transfers between devices, relay(): lax.ppermute(left[:half], axis, RIGHT)  17.7 us
    all_to_all x2, starting transfers between devices, exchange(): return lax.all_to_all(terms, plane, split_axis=0, concat_axis=0, tiled=True)  14.3 us
    dot_general x4, matrix products, backward(): lax.dot_general(grad, weight, (((1,), (1,)), ((), ())), preferred_element...  14.1 us
    dot_general x4, matrix products, forward(): out = jnp.dot(act.reshape(16 * sub, ff), weight, preferred_element_type=f32)  11.5 us
    all_to_all x2, waiting for transfers between devices, exchange(): return lax.all_to_all(terms, plane, split_axis=0, concat_axis=0, tiled=True)  7.87 us
    dynamic_update_slice x6, local copies, waits for them, and re-layouts, place(): out = lax.dynamic_update_slice(out, jnp.expand_dims(block, dim), at)  7.56 us
  transfers between devices with their start and end apart: 24, of which 8 were waited for; matrix products, arithmetic and copies ran while one was open for 34% of the time, Pallas kernels for 5%

commit v1 on v0

--- a/solution.py
+++ b/solution.py
@@ -1,5 +1,3 @@
-import functools
-
 import jax
 import jax.numpy as jnp
 from jax import lax
@@ -84,9 +82,8 @@
     )(x.astype(jnp.int32).reshape(1), hidden_in)
 
 
-def weight_kernel(scale, at_ref, act_0, act_1, act_2, act_3, grad_0, grad_1, *rest):
-    *other, out_ref, act, grad, total = rest
-    pair = pl.program_id(0)
+def weight_kernel(at_ref, act_0, act_1, act_2, act_3, grad_0, grad_1, give_ref, keep_ref, act, grad, total):
+    half, pair = pl.program_id(0), pl.program_id(1)
     rows = act_0.shape[0]
 
     @pl.when(pair == 0)
@@ -107,43 +104,43 @@
     def _():
         total[...] = term
 
-    @pl.when(pair == 1)
-    def _():
-        done = total[...] + term
-        for ref in other:
-            done = (done + ref[...].astype(f32)) * scale
-        out_ref[...] = done.astype(out_ref.dtype)
-
-
-def weight_sum(acts, places, grad_all, side, other=(), scale=1.0):
+    @pl.when((pair == 1) & (half == 0))
+    def _():
+        give_ref[...] = (total[...] + term).astype(give_ref.dtype)
+
+    @pl.when((pair == 1) & (half == 1))
+    def _():
+        keep_ref[...] = (total[...] + term).astype(keep_ref.dtype)
+
+
+def weight_sums(acts, places, grad_all, core):
     rows, ff = acts[0].shape
     chips, _, sub, cols = grad_all.shape
-    whole = pl.BlockSpec((ff // 2, cols), lambda pair, at_ref: (0, 0))
-    act_spec = pl.BlockSpec((rows, ff // 2), lambda pair, at_ref: (0, at_ref[4]))
+    act_spec = pl.BlockSpec((rows, ff // 2), lambda half, pair, at_ref: (0, lax.rem(at_ref[4] + half + 1, 2)))
     grad_specs = [
-        pl.BlockSpec((chips, 1, sub, cols), lambda pair, at_ref, which=which: (0, at_ref[2 * pair + which], 0, 0))
+        pl.BlockSpec((chips, 1, sub, cols), lambda half, pair, at_ref, which=which: (0, at_ref[2 * pair + which], 0, 0))
         for which in (0, 1)
     ]
     return pl.pallas_call(
-        functools.partial(weight_kernel, scale),
+        weight_kernel,
         grid_spec=pltpu.PrefetchScalarGridSpec(
             num_scalar_prefetch=1,
-            grid=(2,),
-            in_specs=[act_spec] * 4 + grad_specs + [whole] * len(other),
-            out_specs=whole,
+            grid=(2, 2),
+            in_specs=[act_spec] * 4 + grad_specs,
+            out_specs=[pl.BlockSpec((ff // 2, cols), lambda half, pair, at_ref: (0, 0))] * 2,
             scratch_shapes=[
                 pltpu.VMEM((2 * rows, ff // 2), bf16),
                 pltpu.VMEM((2 * rows, cols), bf16),
                 pltpu.VMEM((ff // 2, cols), f32),
             ],
         ),
-        out_shape=jax.ShapeDtypeStruct((ff // 2, cols), bf16),
+        out_shape=[jax.ShapeDtypeStruct((ff // 2, cols), bf16)] * 2,
         compiler_params=pltpu.CompilerParams(vmem_limit_bytes=48 * 2**20),
         cost_estimate=pl.CostEstimate(
-            flops=4 * rows * ff * cols, bytes_accessed=4 * rows * (ff + 2 * cols) + 2 * ff * cols, transcendentals=0
+            flops=8 * rows * ff * cols, bytes_accessed=2 * (4 * rows * (ff + 2 * cols) + ff * cols), transcendentals=0
         ),
-        name="weight_sum",
-    )(jnp.stack([*places, side]).astype(jnp.int32), *acts, grad_all, grad_all, *other)
+        name="weight_sums",
+    )(jnp.stack([*places, core]).astype(jnp.int32), *acts, grad_all, grad_all)
 
 
 def body(hidden_in, down_weight, out_grad):
@@ -232,26 +229,26 @@
     sum_right, sum_left = add(to_right[0], first), add(to_left[1], second)
     sum_right, sum_left = tie(lax.ppermute(sum_right, "x", RIGHT), lax.ppermute(sum_left, "x", LEFT))
     terms_b = exchange(terms_b)
-    home = quarter(grad_late, 0)
+    terms_a, me = tie(terms_a, x)
+    home = backward(at(grad_late, me, 0))
+    sum_right, sum_left, to_right, to_left, grad_late, home = lax.optimization_barrier(
+        (sum_right, sum_left, to_right[1], to_left[0], grad_late, home)
+    )
+
+    term_right, term_left = tie(lax.ppermute(to_right, "x", RIGHT), lax.ppermute(to_left, "x", LEFT))
     acts = [act.reshape(16 * sub, ff) for act in (act_mine, act_left, act_right, act_far)]
-    terms_a, other_core = tie(terms_a, 1 - core)
-    give_sum = weight_sum(acts, places, grad_late.reshape(16, 4, sub, cols), other_core)
-    sum_right, sum_left, to_right, to_left, grad_late, home, give_sum = lax.optimization_barrier(
-        (sum_right, sum_left, to_right[1], to_left[0], grad_late, home, give_sum)
-    )
-
-    term_right, term_left = tie(lax.ppermute(to_right, "x", RIGHT), lax.ppermute(to_left, "x", LEFT))
+    give_sum, keep_sum = weight_sums(acts, places, grad_late.reshape(16, 4, sub, cols), core)
+    term_right, term_left, give_sum, keep_sum = tie(term_right, term_left, give_sum, keep_sum)
+
     take_sum = lax.ppermute(give_sum, "core", SWAP)
-    weight_grad = weight_sum(
-        acts, places, grad_late.reshape(16, 4, sub, cols), core, (take_sum,), float(32 * tok) ** (-0.5)
-    )
-    term_right, term_left, weight_grad = tie(term_right, term_left, weight_grad)
+    weight_grad = (keep_sum.astype(f32) + take_sum.astype(f32)) * float(32 * tok) ** (-0.5)
+    weight_grad = weight_grad.astype(bf16)
 
     slope = gelu_slope(rows.reshape(4 * tok, ff).astype(f32))
     from_left = jnp.concatenate([sum_right, term_right]).astype(f32)
     from_right = jnp.concatenate([term_left, sum_left]).astype(f32)
     summed = home.reshape(4 * tok, ff).astype(f32) + from_left + from_right
-    (grad_here,) = tie((summed * slope).astype(bf16).reshape(4, 1, tok, ff))
+    grad_here, terms_b = tie((summed * slope).astype(bf16).reshape(4, 1, tok, ff), terms_b)
     keep = lax.dynamic_slice(grad_here, (0, 0, 0, ff_dev * core), (4, 1, tok, ff_dev))
     give = lax.dynamic_slice(grad_here, (0, 0, 0, ff_dev * (1 - core)), (4, 1, tok, ff_dev))
     take = lax.ppermute(give, "core", SWAP)

time: 228 us -> 214 us (0.939)
  local copies, waits for them, and re-layouts: 37.5 us -> 28.2 us
  Pallas kernels: 25.2 us -> 21.4 us
  waiting for transfers between devices: 52 us -> 48.7 us
    ppermute x1, waiting for transfers between devices: 0.01 us -> 9.56 us  [body(): lax.ppermute(sum_right, 'x', RIGHT)]
    all_to_all x2, waiting for transfers between devices: 7.87 us -> 0.01 us  [exchange(): return lax.all_to_all(terms, plane, split_axis=0, concat_axis=0, tiled=True)]
    ppermute x1, waiting for transfers between devices: 5.73 us -> 0.01 us  [body(): lax.ppermute(to_right, 'x', RIGHT)]
    convert_element_type x1 -> x2, other arithmetic: 3.76 us -> 8.08 us  [the longest x1 4.33 us: body(): weight_grad = weight_grad.astype(bf16)]
    unnamed x31 -> x35, local copies, waits for them, and re-layouts: 7.07 us -> 3.05 us
    pallas_call x2 -> x1, Pallas kernels: 21.6 us -> 17.8 us  [weight_sums(): pl.pallas_call(weight_kernel, grid_spec=pltpu.PrefetchScalarGridSpec(num_...]
    ppermute x1, starting transfers between devices: 2.87 us -> 0.1 us  [body(): take = lax.ppermute(give, 'core', SWAP)]
  transfers between devices with their start and end apart: 24 -> 24, of which waited for: 8 -> 8; matrix products, arithmetic and copies ran while one was open for 34% -> 36% of each run, Pallas kernels for 5% -> 8%
where the time goes in v1:
time: 214 us; the launch traced here: 213 us
  starting transfers between devices  56.3 us (26%)
  waiting for transfers between devices  48.7 us (23%)
  other arithmetic  30.5 us (14%)
  local copies, waits for them, and re-layouts  28.2 us (13%)
  matrix products  27 us (13%)
  Pallas kernels  21.4 us (10%)
    ppermute x3, waiting for transfers between devices, shift(): lax.ppermute(block, axis, RIGHT)  20.9 us
    pallas_call x1, Pallas kernels, weight_sums(): pl.pallas_call(weight_kernel, grid_spec=pltpu.PrefetchScalarGridSpec(num_...  17.8 us
    ppermute x3, waiting for transfers between devices, relay(): lax.ppermute(left[:half], axis, RIGHT)  17.1 us
    dot_general x4, matrix products, backward(): lax.dot_general(grad, weight, (((1,), (1,)), ((), ())), preferred_element...  15.4 us
    all_to_all x2, starting transfers between devices, exchange(): return lax.all_to_all(terms, plane, split_axis=0, concat_axis=0, tiled=True)  13.1 us
    dot_general x4, matrix products, forward(): out = jnp.dot(act.reshape(16 * sub, ff), weight, preferred_element_type=f32)  11.5 us
    ppermute x1, waiting for transfers between devices, body(): lax.ppermute(sum_right, 'x', RIGHT)  9.56 us
    ppermute x1, starting transfers between devices, body(): take_sum = lax.ppermute(give_sum, 'core', SWAP)  8.07 us
  transfers between devices with their start and end apart: 24, of which 8 were waited for; matrix products, arithmetic and copies ran while one was open for 36% of the time, Pallas kernels for 8%

profile of v1, /device:TPU:1, one launch (start us, length us, event | category | flops | bytes accessed | tf_op | source)
XLA Modules:
  0.0 213.2 jit_solution(8990706056092993550)
XLA Ops:
  0.6 3.6 %split_quarter.1 = bf16[16,32,1536]{2,1,0:T(8,128)(2,1)} custom-call(s32[1]{0:T(128)} %bitcast.x_ref, bf16[128,24576]{1,0:T(8,128)(2,1)} %rows_ref.1), custom_call_target="tpu_custom_call" | custom-call | tf_op jit(solution)/shard_map/split_quarter/pallas_call | solution.py:72
  4.2 2.5 %collective-permute-start.2 = (bf16[128,1536]{1,0:T(8,128)(2,1)}, bf16[128,1536]{1,0:T(8,128)(2,1)S(1)}, u32[]{:S(2)}, u32[]{:S(2)}) collective-permute-start(bf16[128,1536]{1,0:T(8,128)(2,1)} %param.5), channel_id=1, source_target_pairs={{0,8},{8,16},{16,24},{24,0},{1,9},{9,17},{17,25},{25,1},{2,10},{10... | collective-permute-start | bytes 1179656 | tf_op jit(solution)/shard_map/ppermute | solution.py:36
  8.8 5.5 %all-to-all-start = ((bf16[16,32,1536]{2,1,0:T(8,128)(2,1)}), bf16[16,32,1536]{2,1,0:T(8,128)(2,1)S(1)}, u32[]{:S(2)}, u32[]{:S(2)}) async-start(bf16[16,32,1536]{2,1,0:T(8,128)(2,1)} %split_quarter.1), calls=%async_computation | async-start | bytes 3145728 | tf_op jit(solution)/shard_map/all_to_all | solution.py:157
  22.7 16.6 %collective-permute-done.4 = bf16[64,1536]{1,0:T(8,128)(2,1)S(1)} collective-permute-done((bf16[64,1536]{1,0:T(8,128)(2,1)S(1)}, bf16[64,1536]{1,0:T(8,128)(2,1)S(1)}, u32[]{:S(2)}, u32[]{:S(2)}) %collective-permute-start.4) | collective-permute-done | bytes 196640 | tf_op jit(solution)/shard_map/ppermute | solution.py:41
  40.7 2.3 %collective-permute-start.1 = (bf16[4,4,32,1536]{3,2,1,0:T(8,128)(2,1)S(1)}, bf16[4,4,32,1536]{3,2,1,0:T(8,128)(2,1)S(1)}, u32[]{:S(2)}, u32[]{:S(2)}) collective-permute-start(bf16[4,4,32,1536]{3,2,1,0:T(8,128)(2,1)S(1)} %bitcast.120), channel_id=1, source_target_pairs={{0,3},{1,0},{2,1},{3,2},{4,7},{5,4},{6,5},{7,6},{8,11},{9,8},{10,9... | collective-permute-start | bytes 4718600 | tf_op jit(solution)/shard_map/ppermute | solution.py:36
  48.8 3.9 %maximum_select_fusion = bf16[1536,1536]{1,0:T(8,128)(2,1)S(1)} fusion(bf16[768,1536]{1,0:T(8,128)(2,1)} %collective-permute-done.6, bf16[768,1536]{1,0:T(8,128)(2,1)S(1)} %copy-done.6, pred[]{:T(512)S(6)} %eq.3), kind=kLoop, calls=%fused_computation.27 | loop fusion | flops 21233664 | bytes 9437185 | tf_op jit(solution)/shard_map/jit(_where)/select_n | solution.py:191
  52.8 2.6 %convolution_convert_fusion.7 = bf16[512,1536]{1,0:T(8,128)(2,1)S(1)} fusion(bf16[512,1536]{1,0:T(8,128)(2,1)S(1)} %bitcast.113, bf16[1536,1536]{1,0:T(8,128)(2,1)S(1)} %maximum_select_fusion), kind=kOutput, calls=%fused_computation.69 | convolution fusion | flops 2416705536 | bytes 7864320 | tf_op jit(solution)/shard_map/dot_general | solution.py:171
  55.4 3.3 %broadcast_in_dim.61 = bf16[4,4,128,1536]{3,2,1,0:T(8,128)(2,1)} broadcast(bf16[]{:T(256)} %constant.82.clone.1), dimensions={} | broadcast | bytes 6291458 | tf_op jit(solution)/shard_map/broadcast_in_dim | solution.py:47
  60.0 15.8 %collective-permute-done = bf16[4,4,32,1536]{3,2,1,0:T(8,128)(2,1)S(1)} collective-permute-done((bf16[4,4,32,1536]{3,2,1,0:T(8,128)(2,1)S(1)}, bf16[4,4,32,1536]{3,2,1,0:T(8,128)(2,1)S(1)}, u32[]{:S(2)}, u32[]{:S(2)}) %collective-permute-start) | collective-permute-done | bytes 1572896 | tf_op jit(solution)/shard_map/ppermute | solution.py:36
  75.9 4.4 %collective-permute-done.7 = bf16[4,128,1536]{2,1,0:T(8,128)(2,1)S(1)} collective-permute-done((bf16[4,128,1536]{2,1,0:T(8,128)(2,1)S(1)}, bf16[4,128,1536]{2,1,0:T(8,128)(2,1)S(1)}, u32[]{:S(2)}, u32[]{:S(2)}) %collective-permute-start.7) | collective-permute-done | bytes 1572896 | tf_op jit(solution)/shard_map/ppermute | solution.py:36
  82.7 2.7 %collective-permute-start.10 = (bf16[2,4,32,1536]{3,2,1,0:T(8,128)(2,1)S(1)}, bf16[2,4,32,1536]{3,2,1,0:T(8,128)(2,1)}, u32[]{:S(2)}, u32[]{:S(2)}) collective-permute-start(bf16[2,4,32,1536]{3,2,1,0:T(8,128)(2,1)S(1)} %slice.51), channel_id=1, source_target_pairs={{0,3},{1,0},{2,1},{3,2},{4,7},{5,4},{6,5},{7,6},{8,11},{9,8},{10,9... | collective-permute-start | bytes 2359304 | tf_op jit(solution)/shard_map/ppermute | solution.py:41
  86.1 2.4 %collective-permute-start.12 = (bf16[2,128,1536]{2,1,0:T(8,128)(2,1)S(1)}, bf16[2,128,1536]{2,1,0:T(8,128)(2,1)S(1)}, u32[]{:S(2)}, u32[]{:S(2)}) collective-permute-start(bf16[2,128,1536]{2,1,0:T(8,128)(2,1)S(1)} %slice.53), channel_id=1, source_target_pairs={{0,96},{32,0},{64,32},{96,64},{1,97},{33,1},{65,33},{97,65},{2,98}... | collective-permute-start | bytes 2359304 | tf_op jit(solution)/shard_map/ppermute | solution.py:41
  88.5 2.6 %convolution_convert_fusion.6 = bf16[512,1536]{1,0:T(8,128)(2,1)S(1)} fusion(bf16[512,1536]{1,0:T(8,128)(2,1)S(1)} %bitcast.115, bf16[1536,1536]{1,0:T(8,128)(2,1)S(1)} %maximum_select_fusion), kind=kOutput, calls=%fused_computation.68 | convolution fusion | flops 2416705536 | bytes 7864320 | tf_op jit(solution)/shard_map/dot_general | solution.py:171
  91.1 3.7 %convolution_convert_fusion.5 = bf16[512,1536]{1,0:T(8,128)(2,1)} fusion(bf16[512,1536]{1,0:T(8,128)(2,1)S(1)} %bitcast.117, bf16[1536,1536]{1,0:T(8,128)(2,1)S(1)} %maximum_select_fusion), kind=kOutput, calls=%fused_computation.67 | convolution fusion | flops 2416705536 | bytes 7864320 | tf_op jit(solution)/shard_map/dot_general | solution.py:171
  103.2 6.7 %all-to-all-start.1 = ((bf16[16,2,32,1536]{3,2,1,0:T(8,128)(2,1)}), bf16[16,2,32,1536]{3,2,1,0:T(8,128)(2,1)}, u32[]{:S(2)}, u32[]{:S(2)}) async-start(bf16[16,2,32,1536]{3,2,1,0:T(8,128)(2,1)} %pad_maximum_fusion), calls=%async_computation.1 | async-start | bytes 6291456 | tf_op jit(solution)/shard_map/all_to_all | solution.py:182
  109.9 2.6 %fusion.29 = bf16[4,4,128,1536]{3,2,1,0:T(8,128)(2,1)} fusion(bf16[4,4,128,1536]{3,2,1,0:T(8,128)(2,1)} %bitcast_dynamic-update-slice_fusion, s32[]{:T(128)S(6)} %select_n.87, bf16[2,128,1536]{2,1,0:T(8,128)(2,1)} %copy-done.13, bf16[2,128,1536]{2,1,0:T(8,128)(2,1)} %copy-done.12), kind=kLoop, calls=%fused_computation.71 | loop fusion | flops 3145728 | bytes 3145732 | tf_op jit(solution)/shard_map/dynamic_update_slice | solution.py:51
  114.2 5.1 %convolution_convert_fusion.4 = bf16[512,1536]{1,0:T(8,128)(2,1)S(1)} fusion(bf16[512,1536]{1,0:T(8,128)(2,1)S(1)} %bitcast.140, bf16[1536,1536]{1,0:T(8,128)(2,1)} %copy-done.4), kind=kOutput, calls=%fused_computation.66 | convolution fusion | flops 2416705536 | bytes 7864320 | tf_op jit(solution)/shard_map/dot_general | solution.py:177
  119.4 2.7 %collective-permute-start.14 = (bf16[256,1536]{1,0:T(8,128)(2,1)S(1)}, bf16[256,1536]{1,0:T(8,128)(2,1)S(1)}, u32[]{:S(2)}, u32[]{:S(2)}) collective-permute-start(bf16[256,1536]{1,0:T(8,128)(2,1)S(1)} %get-tuple-element.141), channel_id=1, source_target_pairs={{0,3},{1,0},{2,1},{3,2},{4,7},{5,4},{6,5},{7,6},{8,11},{9,8},{10,9... | collective-permute-start | bytes 2359304 | tf_op jit(solution)/shard_map/ppermute | solution.py:219
  124.2 2.6 %convolution_convert_fusion.3 = bf16[512,1536]{1,0:T(8,128)(2,1)S(1)} fusion(bf16[512,1536]{1,0:T(8,128)(2,1)S(1)} %bitcast.143, bf16[1536,1536]{1,0:T(8,128)(2,1)S(1)} %bitcast.126), kind=kOutput, calls=%fused_computation.65 | convolution fusion | flops 2416705536 | bytes 7864320 | tf_op jit(solution)/shard_map/dot_general | solution.py:177
  126.9 2.6 %convolution_convert_fusion.2 = bf16[512,1536]{1,0:T(8,128)(2,1)S(1)} fusion(bf16[512,1536]{1,0:T(8,128)(2,1)S(1)} %bitcast.142, bf16[1536,1536]{1,0:T(8,128)(2,1)S(1)} %bitcast.126), kind=kOutput, calls=%fused_computation.64 | convolution fusion | flops 2416705536 | bytes 7864320 | tf_op jit(solution)/shard_map/dot_general | solution.py:177
  133.0 2.6 %convolution_convert_fusion.1 = bf16[512,1536]{1,0:T(8,128)(2,1)S(1)} fusion(bf16[512,1536]{1,0:T(8,128)(2,1)S(1)} %bitcast.127, bf16[1536,1536]{1,0:T(8,128)(2,1)S(1)} %bitcast.126), kind=kOutput, calls=%fused_computation.63 | convolution fusion | flops 2416705536 | bytes 7864320 | tf_op jit(solution)/shard_map/dot_general | solution.py:171
  138.8 2.7 %collective-permute-start.16 = (bf16[256,1536]{1,0:T(8,128)(2,1)S(1)}, bf16[256,1536]{1,0:T(8,128)(2,1)}, u32[]{:S(2)}, u32[]{:S(2)}) collective-permute-start(bf16[256,1536]{1,0:T(8,128)(2,1)S(1)} %fusion.30), channel_id=1, source_target_pairs={{0,3},{1,0},{2,1},{3,2},{4,7},{5,4},{6,5},{7,6},{8,11},{9,8},{10,9... | collective-permute-start | bytes 2359304 | tf_op jit(solution)/shard_map/ppermute | solution.py:230
  143.5 9.6 %collective-permute-done.15 = bf16[256,1536]{1,0:T(8,128)(2,1)} collective-permute-done((bf16[256,1536]{1,0:T(8,128)(2,1)S(1)}, bf16[256,1536]{1,0:T(8,128)(2,1)}, u32[]{:S(2)}, u32[]{:S(2)}) %collective-permute-start.15) | collective-permute-done | bytes 786464 | tf_op jit(solution)/shard_map/ppermute | solution.py:230
  153.0 6.4 %all-to-all-start.2 = ((bf16[16,2,32,1536]{3,2,1,0:T(8,128)(2,1)}), bf16[16,2,32,1536]{3,2,1,0:T(8,128)(2,1)}, u32[]{:S(2)}, u32[]{:S(2)}) async-start(bf16[16,2,32,1536]{3,2,1,0:T(8,128)(2,1)} %pad_maximum_fusion.1), calls=%async_computation.2 | async-start | bytes 6291456 | tf_op jit(solution)/shard_map/all_to_all | solution.py:182
  159.4 2.4 %reduce_sum.24 = bf16[2,32,1536]{2,1,0:T(8,128)(2,1)S(1)} reduce(bf16[16,2,32,1536]{3,2,1,0:T(8,128)(2,1)} %all-to-all-done.1, bf16[]{:T(256)} %constant.82.clone.1), dimensions={0}, to_apply=%region_0.1 | reduce | flops 1474560 | bytes 3342338 | tf_op jit(solution)/shard_map/reduce_sum | solution.py:262
  163.3 5.1 %convolution_convert_fusion = bf16[512,1536]{1,0:T(8,128)(2,1)S(1)} fusion(bf16[512,1536]{1,0:T(8,128)(2,1)S(1)} %bitcast.139, bf16[1536,1536]{1,0:T(8,128)(2,1)} %copy-done.4), kind=kOutput, calls=%fused_computation.62 | convolution fusion | flops 2416705536 | bytes 7864320 | tf_op jit(solution)/shard_map/dot_general | solution.py:177
  168.6 2.9 %collective-permute-start.18 = (bf16[256,1536]{1,0:T(8,128)(2,1)S(1)}, bf16[256,1536]{1,0:T(8,128)(2,1)S(1)}, u32[]{:S(2)}, u32[]{:S(2)}) collective-permute-start(bf16[256,1536]{1,0:T(8,128)(2,1)S(1)} %copy-done.10), channel_id=1, source_target_pairs={{0,3},{1,0},{2,1},{3,2},{4,7},{5,4},{6,5},{7,6},{8,11},{9,8},{10,9... | collective-permute-start | bytes 2359304 | tf_op jit(solution)/shard_map/ppermute | solution.py:238
  171.6 17.8 %weight_sums.1 = (bf16[768,1536]{1,0:T(8,128)(2,1)}, bf16[768,1536]{1,0:T(8,128)(2,1)}) custom-call(s32[5]{0:T(128)S(1)} %stack.23.at_ref, bf16[512,1536]{1,0:T(8,128)(2,1)S(1)} %bitcast.114, bf16[512,1536]{1,0:T(8,128)(2,1)S(1)} %bitcast.116, bf16[512,1536]{1,0:T(8,128)(2,1)S(1)} %bitcast.118, bf16[512,1536]{1,0:T(8,128)(2,1)} %bitcast.128, ...), custom_call_target="tpu_custom_call" | custom-call | flops 9663676416 | bytes 23592960 | tf_op jit(solution)/shard_map/weight_sums/pallas_call | solution.py:124
  189.5 8.1 %collective-permute-start.20 = (bf16[768,1536]{1,0:T(8,128)(2,1)}, bf16[768,1536]{1,0:T(8,128)(2,1)}, u32[]{:S(2)}, u32[]{:S(2)}) collective-permute-start(bf16[768,1536]{1,0:T(8,128)(2,1)} %get-tuple-element.136), channel_id=1, source_target_pairs={{0,4},{4,0},{1,5},{5,1},{2,6},{6,2},{3,7},{7,3},{8,12},{12,8},{9,1... | collective-permute-start | bytes 7077896 | tf_op jit(solution)/shard_map/ppermute | solution.py:243
  200.0 3.8 %fusion.27 = bf16[4,1,128,1536]{3,2,1,0:T(8,128)(2,1)S(1)} fusion(bf16[4,1,128,1536]{3,2,1,0:T(8,128)(2,1)S(1)} %bitcast.123, bf16[4,1,128,1536]{3,2,1,0:T(8,128)(2,1)S(1)} %bitcast.124, bf16[4,1,128,1536]{3,2,1,0:T(8,128)(2,1)S(1)} %bitcast.141, bf16[4,1,128,1536]{3,2,1,0:T(8,128)(2,1)} %bitcast.112), kind=kLoop, calls=%fused_computation.56 | loop fusion | flops 19660800 | bytes 7864320 | tf_op jit(solution)/shard_map/convert_element_type | solution.py:251
  203.8 2.4 %reduce_sum.25 = bf16[2,32,1536]{2,1,0:T(8,128)(2,1)S(1)} reduce(bf16[16,2,32,1536]{3,2,1,0:T(8,128)(2,1)} %all-to-all-done.2, bf16[]{:T(256)} %constant.82.clone.1), dimensions={0}, to_apply=%region_1.2 | reduce | flops 1474560 | bytes 3342338 | tf_op jit(solution)/shard_map/reduce_sum | solution.py:262
  208.9 4.3 %multiply_convert_fusion = bf16[768,1536]{1,0:T(8,128)(2,1)} fusion(bf16[768,1536]{1,0:T(8,128)(2,1)} %collective-permute-done.20, bf16[768,1536]{1,0:T(8,128)(2,1)S(1)} %copy-done.5), kind=kLoop, calls=%fused_computation.28 | loop fusion | flops 5898240 | bytes 7077888 | tf_op jit(solution)/shard_map/convert_element_type | solution.py:245
  (113 shorter events, 49.8 us)
Async XLA Ops:
  4.2 13.6 %collective-permute-start.2 = (bf16[128,1536]{1,0:T(8,128)(2,1)}, bf16[128,1536]{1,0:T(8,128)(2,1)S(1)}, u32[]{:S(2)}, u32[]{:S(2)}) collective-permute-start(bf16[128,1536]{1,0:T(8,128)(2,1)} %param.5), channel_id=1, source_target_pairs={{0,8},{8,16},{16,24},{24,0},{1,9},{9,17},{17,25},{25,1},{2,10},{10... | collective-permute-start | bytes 1179656 | tf_op jit(solution)/shard_map/ppermute | solution.py:36
  6.7 11.2 %collective-permute-start.3 = (bf16[128,1536]{1,0:T(8,128)(2,1)}, bf16[128,1536]{1,0:T(8,128)(2,1)}, u32[]{:S(2)}, u32[]{:S(2)}) collective-permute-start(bf16[128,1536]{1,0:T(8,128)(2,1)} %param.5), channel_id=1, source_target_pairs={{0,24},{8,0},{16,8},{24,16},{1,25},{9,1},{17,9},{25,17},{2,26},{10... | collective-permute-start | bytes 1179656 | tf_op jit(solution)/shard_map/ppermute | solution.py:36
  8.8 30.6 %all-to-all-start = ((bf16[16,32,1536]{2,1,0:T(8,128)(2,1)}), bf16[16,32,1536]{2,1,0:T(8,128)(2,1)S(1)}, u32[]{:S(2)}, u32[]{:S(2)}) async-start(bf16[16,32,1536]{2,1,0:T(8,128)(2,1)} %split_quarter.1), calls=%async_computation | async-start | bytes 3145728 | tf_op jit(solution)/shard_map/all_to_all | solution.py:157
  14.3 31.9 %collective-permute-start.6 = (bf16[768,1536]{1,0:T(8,128)(2,1)}, bf16[768,1536]{1,0:T(8,128)(2,1)}, u32[]{:S(2)}, u32[]{:S(2)}) collective-permute-start(bf16[768,1536]{1,0:T(8,128)(2,1)} %param.4), channel_id=1, source_target_pairs={{0,4},{4,0},{1,5},{5,1},{2,6},{6,2},{3,7},{7,3},{8,12},{12,8},{9,1... | collective-permute-start | bytes 7077896 | tf_op jit(solution)/shard_map/ppermute | solution.py:163
  17.9 21.4 %collective-permute-start.4 = (bf16[64,1536]{1,0:T(8,128)(2,1)S(1)}, bf16[64,1536]{1,0:T(8,128)(2,1)S(1)}, u32[]{:S(2)}, u32[]{:S(2)}) collective-permute-start(bf16[64,1536]{1,0:T(8,128)(2,1)S(1)} %slice.48), channel_id=1, source_target_pairs={{0,8},{8,16},{16,24},{24,0},{1,9},{9,17},{17,25},{25,1},{2,10},{10... | collective-permute-start | bytes 589832 | tf_op jit(solution)/shard_map/ppermute | solution.py:41
  19.7 19.6 %collective-permute-start.5 = (bf16[64,1536]{1,0:T(8,128)(2,1)S(1)}, bf16[64,1536]{1,0:T(8,128)(2,1)S(1)}, u32[]{:S(2)}, u32[]{:S(2)}) collective-permute-start(bf16[64,1536]{1,0:T(8,128)(2,1)S(1)} %slice.49), channel_id=1, source_target_pairs={{0,24},{8,0},{16,8},{24,16},{1,25},{9,1},{17,9},{25,17},{2,26},{10... | collective-permute-start | bytes 589832 | tf_op jit(solution)/shard_map/ppermute | solution.py:41
  39.4 9.5 %copy-start.6 = (bf16[768,1536]{1,0:T(8,128)(2,1)S(1)}, bf16[768,1536]{1,0:T(8,128)(2,1)}, u32[]{:S(2)}) copy-start(bf16[768,1536]{1,0:T(8,128)(2,1)} %param.4) | copy-start | bytes 7077892
  39.4 36.4 %collective-permute-start = (bf16[4,4,32,1536]{3,2,1,0:T(8,128)(2,1)S(1)}, bf16[4,4,32,1536]{3,2,1,0:T(8,128)(2,1)S(1)}, u32[]{:S(2)}, u32[]{:S(2)}) collective-permute-start(bf16[4,4,32,1536]{3,2,1,0:T(8,128)(2,1)S(1)} %bitcast.119), channel_id=1, source_target_pairs={{0,1},{1,2},{2,3},{3,0},{4,5},{5,6},{6,7},{7,4},{8,9},{9,10},{10,1... | collective-permute-start | bytes 4718600 | tf_op jit(solution)/shard_map/ppermute | solution.py:36
  40.7 35.2 %collective-permute-start.1 = (bf16[4,4,32,1536]{3,2,1,0:T(8,128)(2,1)S(1)}, bf16[4,4,32,1536]{3,2,1,0:T(8,128)(2,1)S(1)}, u32[]{:S(2)}, u32[]{:S(2)}) collective-permute-start(bf16[4,4,32,1536]{3,2,1,0:T(8,128)(2,1)S(1)} %bitcast.120), channel_id=1, source_target_pairs={{0,3},{1,0},{2,1},{3,2},{4,7},{5,4},{6,5},{7,6},{8,11},{9,8},{10,9... | collective-permute-start | bytes 4718600 | tf_op jit(solution)/shard_map/ppermute | solution.py:36
  46.2 34.1 %collective-permute-start.7 = (bf16[4,128,1536]{2,1,0:T(8,128)(2,1)S(1)}, bf16[4,128,1536]{2,1,0:T(8,128)(2,1)S(1)}, u32[]{:S(2)}, u32[]{:S(2)}) collective-permute-start(bf16[4,128,1536]{2,1,0:T(8,128)(2,1)S(1)} %copy-done.3), channel_id=1, source_target_pairs={{0,32},{32,64},{64,96},{96,0},{1,33},{33,65},{65,97},{97,1},{2,34}... | collective-permute-start | bytes 4718600 | tf_op jit(solution)/shard_map/ppermute | solution.py:36
  47.3 32.9 %collective-permute-start.8 = (bf16[4,128,1536]{2,1,0:T(8,128)(2,1)S(1)}, bf16[4,128,1536]{2,1,0:T(8,128)(2,1)S(1)}, u32[]{:S(2)}, u32[]{:S(2)}) collective-permute-start(bf16[4,128,1536]{2,1,0:T(8,128)(2,1)S(1)} %copy-done.3), channel_id=1, source_target_pairs={{0,96},{32,0},{64,32},{96,64},{1,97},{33,1},{65,33},{97,65},{2,98}... | collective-permute-start | bytes 4718600 | tf_op jit(solution)/shard_map/ppermute | solution.py:36
  52.8 38.3 %copy-start.4 = (bf16[1536,1536]{1,0:T(8,128)(2,1)}, bf16[1536,1536]{1,0:T(8,128)(2,1)S(1)}, u32[]{:S(2)}) copy-start(bf16[1536,1536]{1,0:T(8,128)(2,1)S(1)} %maximum_select_fusion) | copy-start | bytes 14155780
  82.6 8.5 %copy-start = (bf16[4,4,32,1536]{3,2,1,0:T(8,128)(2,1)}, bf16[4,4,32,1536]{3,2,1,0:T(8,128)(2,1)S(1)}, u32[]{:S(2)}) copy-start(bf16[4,4,32,1536]{3,2,1,0:T(8,128)(2,1)S(1)} %get-tuple-element.123) | copy-start | bytes 4718596
  82.6 18.3 %collective-permute-start.9 = (bf16[2,4,32,1536]{3,2,1,0:T(8,128)(2,1)S(1)}, bf16[2,4,32,1536]{3,2,1,0:T(8,128)(2,1)}, u32[]{:S(2)}, u32[]{:S(2)}) collective-permute-start(bf16[2,4,32,1536]{3,2,1,0:T(8,128)(2,1)S(1)} %slice.50), channel_id=1, source_target_pairs={{0,1},{1,2},{2,3},{3,0},{4,5},{5,6},{6,7},{7,4},{8,9},{9,10},{10,1... | collective-permute-start | bytes 2359304 | tf_op jit(solution)/shard_map/ppermute | solution.py:41
  82.7 18.2 %collective-permute-start.10 = (bf16[2,4,32,1536]{3,2,1,0:T(8,128)(2,1)S(1)}, bf16[2,4,32,1536]{3,2,1,0:T(8,128)(2,1)}, u32[]{:S(2)}, u32[]{:S(2)}) collective-permute-start(bf16[2,4,32,1536]{3,2,1,0:T(8,128)(2,1)S(1)} %slice.51), channel_id=1, source_target_pairs={{0,3},{1,0},{2,1},{3,2},{4,7},{5,4},{6,5},{7,6},{8,11},{9,8},{10,9... | collective-permute-start | bytes 2359304 | tf_op jit(solution)/shard_map/ppermute | solution.py:41
  85.4 16.0 %collective-permute-start.11 = (bf16[2,128,1536]{2,1,0:T(8,128)(2,1)S(1)}, bf16[2,128,1536]{2,1,0:T(8,128)(2,1)S(1)}, u32[]{:S(2)}, u32[]{:S(2)}) collective-permute-start(bf16[2,128,1536]{2,1,0:T(8,128)(2,1)S(1)} %slice.52), channel_id=1, source_target_pairs={{0,32},{32,64},{64,96},{96,0},{1,33},{33,65},{65,97},{97,1},{2,34}... | collective-permute-start | bytes 2359304 | tf_op jit(solution)/shard_map/ppermute | solution.py:41
  86.1 15.3 %collective-permute-start.12 = (bf16[2,128,1536]{2,1,0:T(8,128)(2,1)S(1)}, bf16[2,128,1536]{2,1,0:T(8,128)(2,1)S(1)}, u32[]{:S(2)}, u32[]{:S(2)}) collective-permute-start(bf16[2,128,1536]{2,1,0:T(8,128)(2,1)S(1)} %slice.53), channel_id=1, source_target_pairs={{0,96},{32,0},{64,32},{96,64},{1,97},{33,1},{65,33},{97,65},{2,98}... | collective-permute-start | bytes 2359304 | tf_op jit(solution)/shard_map/ppermute | solution.py:41
  103.2 49.8 %all-to-all-start.1 = ((bf16[16,2,32,1536]{3,2,1,0:T(8,128)(2,1)}), bf16[16,2,32,1536]{3,2,1,0:T(8,128)(2,1)}, u32[]{:S(2)}, u32[]{:S(2)}) async-start(bf16[16,2,32,1536]{3,2,1,0:T(8,128)(2,1)} %pad_maximum_fusion), calls=%async_computation.1 | async-start | bytes 6291456 | tf_op jit(solution)/shard_map/all_to_all | solution.py:182
  112.5 11.7 %slice-start = ((s8[4718592]{0:T(1024)(128)(4,1)}), s8[4194304]{0:T(1024)(128)(4,1)S(1)}, s32[]{:S(2)}) async-start(s8[4718592]{0:T(1024)(128)(4,1)} %bitcast.125), calls=%async_computation.3 | async-start | bytes 8388608
  114.2 10.1 %slice-start.1 = ((s8[4718592]{0:T(1024)(128)(4,1)}), s8[524288]{0:T(1024)(128)(4,1)S(1)}, s32[]{:S(2)}) async-start(s8[4718592]{0:T(1024)(128)(4,1)} %bitcast.125), calls=%async_computation.4 | async-start | bytes 1048576
  119.4 19.0 %collective-permute-start.13 = (bf16[256,1536]{1,0:T(8,128)(2,1)S(1)}, bf16[256,1536]{1,0:T(8,128)(2,1)S(1)}, u32[]{:S(2)}, u32[]{:S(2)}) collective-permute-start(bf16[256,1536]{1,0:T(8,128)(2,1)S(1)} %get-tuple-element.142), channel_id=1, source_target_pairs={{0,1},{1,2},{2,3},{3,0},{4,5},{5,6},{6,7},{7,4},{8,9},{9,10},{10,1... | collective-permute-start | bytes 2359304 | tf_op jit(solution)/shard_map/ppermute | solution.py:219
  119.4 18.9 %collective-permute-start.14 = (bf16[256,1536]{1,0:T(8,128)(2,1)S(1)}, bf16[256,1536]{1,0:T(8,128)(2,1)S(1)}, u32[]{:S(2)}, u32[]{:S(2)}) collective-permute-start(bf16[256,1536]{1,0:T(8,128)(2,1)S(1)} %get-tuple-element.141), channel_id=1, source_target_pairs={{0,3},{1,0},{2,1},{3,2},{4,7},{5,4},{6,5},{7,6},{8,11},{9,8},{10,9... | collective-permute-start | bytes 2359304 | tf_op jit(solution)/shard_map/ppermute | solution.py:219
  138.6 14.5 %collective-permute-start.15 = (bf16[256,1536]{1,0:T(8,128)(2,1)S(1)}, bf16[256,1536]{1,0:T(8,128)(2,1)}, u32[]{:S(2)}, u32[]{:S(2)}) collective-permute-start(bf16[256,1536]{1,0:T(8,128)(2,1)S(1)} %fusion.31), channel_id=1, source_target_pairs={{0,1},{1,2},{2,3},{3,0},{4,5},{5,6},{6,7},{7,4},{8,9},{9,10},{10,1... | collective-permute-start | bytes 2359304 | tf_op jit(solution)/shard_map/ppermute | solution.py:230
  138.8 14.2 %collective-permute-start.16 = (bf16[256,1536]{1,0:T(8,128)(2,1)S(1)}, bf16[256,1536]{1,0:T(8,128)(2,1)}, u32[]{:S(2)}, u32[]{:S(2)}) collective-permute-start(bf16[256,1536]{1,0:T(8,128)(2,1)S(1)} %fusion.30), channel_id=1, source_target_pairs={{0,3},{1,0},{2,1},{3,2},{4,7},{5,4},{6,5},{7,6},{8,11},{9,8},{10,9... | collective-permute-start | bytes 2359304 | tf_op jit(solution)/shard_map/ppermute | solution.py:230
  153.0 50.8 %all-to-all-start.2 = ((bf16[16,2,32,1536]{3,2,1,0:T(8,128)(2,1)}), bf16[16,2,32,1536]{3,2,1,0:T(8,128)(2,1)}, u32[]{:S(2)}, u32[]{:S(2)}) async-start(bf16[16,2,32,1536]{3,2,1,0:T(8,128)(2,1)} %pad_maximum_fusion.1), calls=%async_computation.2 | async-start | bytes 6291456 | tf_op jit(solution)/shard_map/all_to_all | solution.py:182
  163.3 5.2 %copy-start.10 = (bf16[256,1536]{1,0:T(8,128)(2,1)S(1)}, bf16[256,1536]{1,0:T(8,128)(2,1)}, u32[]{:S(2)}) copy-start(bf16[256,1536]{1,0:T(8,128)(2,1)} %slice_bitcast_fusion) | copy-start | bytes 2359300
  163.3 8.3 %copy-start.1 = (bf16[4,4,32,1536]{3,2,1,0:T(8,128)(2,1)S(1)}, bf16[4,4,32,1536]{3,2,1,0:T(8,128)(2,1)}, u32[]{:S(2)}) copy-start(bf16[4,4,32,1536]{3,2,1,0:T(8,128)(2,1)} %copy-done) | copy-start | bytes 4718596
  168.5 21.0 %collective-permute-start.17 = (bf16[256,1536]{1,0:T(8,128)(2,1)S(1)}, bf16[256,1536]{1,0:T(8,128)(2,1)S(1)}, u32[]{:S(2)}, u32[]{:S(2)}) collective-permute-start(bf16[256,1536]{1,0:T(8,128)(2,1)S(1)} %copy-done.11), channel_id=1, source_target_pairs={{0,1},{1,2},{2,3},{3,0},{4,5},{5,6},{6,7},{7,4},{8,9},{9,10},{10,1... | collective-permute-start | bytes 2359304 | tf_op jit(solution)/shard_map/ppermute | solution.py:238
  168.6 20.9 %collective-permute-start.18 = (bf16[256,1536]{1,0:T(8,128)(2,1)S(1)}, bf16[256,1536]{1,0:T(8,128)(2,1)S(1)}, u32[]{:S(2)}, u32[]{:S(2)}) collective-permute-start(bf16[256,1536]{1,0:T(8,128)(2,1)S(1)} %copy-done.10), channel_id=1, source_target_pairs={{0,3},{1,0},{2,1},{3,2},{4,7},{5,4},{6,5},{7,6},{8,11},{9,8},{10,9... | collective-permute-start | bytes 2359304 | tf_op jit(solution)/shard_map/ppermute | solution.py:238
  171.6 17.9 %copy-start.14 = (bf16[4,32,1536]{2,1,0:T(8,128)(2,1)}, bf16[4,32,1536]{2,1,0:T(8,128)(2,1)S(1)}, u32[]{:S(2)}) copy-start(bf16[4,32,1536]{2,1,0:T(8,128)(2,1)S(1)} %slice_dynamic-update-slice_fusion.2) | copy-start | bytes 1179652
  189.5 19.4 %collective-permute-start.20 = (bf16[768,1536]{1,0:T(8,128)(2,1)}, bf16[768,1536]{1,0:T(8,128)(2,1)}, u32[]{:S(2)}, u32[]{:S(2)}) collective-permute-start(bf16[768,1536]{1,0:T(8,128)(2,1)} %get-tuple-element.136), channel_id=1, source_target_pairs={{0,4},{4,0},{1,5},{5,1},{2,6},{6,2},{3,7},{7,3},{8,12},{12,8},{9,1... | collective-permute-start | bytes 7077896 | tf_op jit(solution)/shard_map/ppermute | solution.py:243
  206.4 2.4 %collective-permute-start.19 = (bf16[4,1,128,768]{3,2,1,0:T(8,128)(2,1)S(1)}, bf16[4,1,128,768]{3,2,1,0:T(8,128)(2,1)S(1)}, u32[]{:S(2)}, u32[]{:S(2)}) collective-permute-start(bf16[4,1,128,768]{3,2,1,0:T(8,128)(2,1)S(1)} %get-tuple-element.139), channel_id=1, source_target_pairs={{0,4},{4,0},{1,5},{5,1},{2,6},{6,2},{3,7},{7,3},{8,12},{12,8},{9,1... | collective-permute-start | bytes 2359304 | tf_op jit(solution)/shard_map/ppermute | solution.py:254
  (9 other events, 24.6 us)

commit v2 on v1

--- a/solution.py
+++ b/solution.py
@@ -229,10 +229,9 @@
     sum_right, sum_left = add(to_right[0], first), add(to_left[1], second)
     sum_right, sum_left = tie(lax.ppermute(sum_right, "x", RIGHT), lax.ppermute(sum_left, "x", LEFT))
     terms_b = exchange(terms_b)
-    terms_a, me = tie(terms_a, x)
-    home = backward(at(grad_late, me, 0))
-    sum_right, sum_left, to_right, to_left, grad_late, home = lax.optimization_barrier(
-        (sum_right, sum_left, to_right[1], to_left[0], grad_late, home)
+    home = quarter(grad_late, 0)
+    sum_right, sum_left, to_right, to_left, grad_late, home, terms_a = lax.optimization_barrier(
+        (sum_right, sum_left, to_right[1], to_left[0], grad_late, home, terms_a)
     )
 
     term_right, term_left = tie(lax.ppermute(to_right, "x", RIGHT), lax.ppermute(to_left, "x", LEFT))

time: 214 us -> 223 us (1.042)
  waiting for transfers between devices: 48.7 us -> 62.3 us
  local copies, waits for them, and re-layouts: 28.2 us -> 17.4 us
  starting transfers between devices: 56.3 us -> 62.3 us
    all_to_all x2, waiting for transfers between devices: 0.01 us -> 12.8 us  [exchange(): return lax.all_to_all(terms, plane, split_axis=0, concat_axis=0, tiled=True)]
    ppermute x1, waiting for transfers between devices: 9.56 us -> 2.78 us  [body(): lax.ppermute(sum_right, 'x', RIGHT)]
    ppermute x3, waiting for transfers between devices: 20.9 us -> 24.8 us  [shift(): lax.ppermute(block, axis, RIGHT)]
    ppermute x3, waiting for transfers between devices: 17.1 us -> 20.7 us  [relay(): lax.ppermute(left[:half], axis, RIGHT)]
    dynamic_slice x3, local copies, waits for them, and re-layouts: 5.26 us -> 1.82 us  [at(): return lax.dynamic_index_in_dim(part, index, dim, keepdims=False)]
    dynamic_update_slice x6, local copies, waits for them, and re-layouts: 5.93 us -> 2.58 us  [place(): out = lax.dynamic_update_slice(out, jnp.expand_dims(block, dim), at)]
    ppermute x1, starting transfers between devices: 0.1 us -> 3.37 us  [body(): take = lax.ppermute(give, 'core', SWAP)]
    broadcast_in_dim x2, local copies, waits for them, and re-layouts: 3.4 us -> 0.72 us  [place(): out = jnp.zeros(shape[:dim] + (4,) + shape[dim:], blocks[0].dtype)]
  transfers between devices with their start and end apart: 24 -> 24, of which waited for: 8 -> 11; matrix products, arithmetic and copies ran while one was open for 36% -> 27% of each run, Pallas kernels for 8% -> 8%
where the time goes in v2:
time: 223 us
  starting transfers between devices  62.3 us (28%)
  waiting for transfers between devices  62.3 us (28%)
  other arithmetic  31.4 us (14%)
  matrix products  26.6 us (12%)
  Pallas kernels  21.4 us (10%)
  local copies, waits for them, and re-layouts  17.4 us (8%)
    ppermute x3, waiting for transfers between devices, shift(): lax.ppermute(block, axis, RIGHT)  24.8 us
    ppermute x3, waiting for transfers between devices, relay(): lax.ppermute(left[:half], axis, RIGHT)  20.7 us
    pallas_call x1, Pallas kernels, weight_sums(): pl.pallas_call(weight_kernel, grid_spec=pltpu.PrefetchScalarGridSpec(num_...  17.8 us
    all_to_all x2, starting transfers between devices, exchange(): return lax.all_to_all(terms, plane, split_axis=0, concat_axis=0, tiled=True)  15.3 us
    dot_general x4, matrix products, backward(): lax.dot_general(grad, weight, (((1,), (1,)), ((), ())), preferred_element...  14 us
    all_to_all x2, waiting for transfers between devices, exchange(): return lax.all_to_all(terms, plane, split_axis=0, concat_axis=0, tiled=True)  12.8 us
    dot_general x4, matrix products, forward(): out = jnp.dot(act.reshape(16 * sub, ff), weight, preferred_element_type=f32)  12.6 us
    ppermute x1, starting transfers between devices, body(): take_sum = lax.ppermute(give_sum, 'core', SWAP)  8.72 us
  transfers between devices with their start and end apart: 24, of which 11 were waited for; matrix products, arithmetic and copies ran while one was open for 27% of the time, Pallas kernels for 8%

profile of v2, /device:TPU:1, one launch (start us, length us, event | category | flops | bytes accessed | tf_op | source)
XLA Modules:
  0.0 222.6 jit_solution(5767916989283700679)
XLA Ops:
  0.6 3.6 %split_quarter.1 = bf16[16,32,1536]{2,1,0:T(8,128)(2,1)} custom-call(s32[1]{0:T(128)} %bitcast.x_ref, bf16[128,24576]{1,0:T(8,128)(2,1)} %rows_ref.1), custom_call_target="tpu_custom_call" | custom-call | tf_op jit(solution)/shard_map/split_quarter/pallas_call | solution.py:72
  4.2 2.5 %collective-permute-start = (bf16[128,1536]{1,0:T(8,128)(2,1)}, bf16[128,1536]{1,0:T(8,128)(2,1)S(1)}, u32[]{:S(2)}, u32[]{:S(2)}) collective-permute-start(bf16[128,1536]{1,0:T(8,128)(2,1)} %param.5), channel_id=1, source_target_pairs={{0,8},{8,16},{16,24},{24,0},{1,9},{9,17},{17,25},{25,1},{2,10},{10... | collective-permute-start | bytes 1179656 | tf_op jit(solution)/shard_map/ppermute | solution.py:36
  8.8 5.5 %all-to-all-start = ((bf16[16,32,1536]{2,1,0:T(8,128)(2,1)}), bf16[16,32,1536]{2,1,0:T(8,128)(2,1)S(1)}, u32[]{:S(2)}, u32[]{:S(2)}) async-start(bf16[16,32,1536]{2,1,0:T(8,128)(2,1)} %split_quarter.1), calls=%async_computation | async-start | bytes 3145728 | tf_op jit(solution)/shard_map/all_to_all | solution.py:157
  22.7 16.6 %collective-permute-done.2 = bf16[64,1536]{1,0:T(8,128)(2,1)S(1)} collective-permute-done((bf16[64,1536]{1,0:T(8,128)(2,1)S(1)}, bf16[64,1536]{1,0:T(8,128)(2,1)S(1)}, u32[]{:S(2)}, u32[]{:S(2)}) %collective-permute-start.2) | collective-permute-done | bytes 196640 | tf_op jit(solution)/shard_map/ppermute | solution.py:41
  47.1 3.9 %maximum_select_fusion = bf16[1536,1536]{1,0:T(8,128)(2,1)S(1)} fusion(bf16[768,1536]{1,0:T(8,128)(2,1)} %collective-permute-done.4, bf16[768,1536]{1,0:T(8,128)(2,1)S(1)} %copy-done.10, pred[]{:T(512)S(6)} %eq.3), kind=kLoop, calls=%fused_computation.27 | loop fusion | flops 21233664 | bytes 9437185 | tf_op jit(solution)/shard_map/jit(_where)/select_n | solution.py:191
  51.0 2.6 %convolution_convert_fusion.7 = bf16[512,1536]{1,0:T(8,128)(2,1)S(1)} fusion(bf16[512,1536]{1,0:T(8,128)(2,1)S(1)} %bitcast.113, bf16[1536,1536]{1,0:T(8,128)(2,1)S(1)} %maximum_select_fusion), kind=kOutput, calls=%fused_computation.69 | convolution fusion | flops 2416705536 | bytes 7864320 | tf_op jit(solution)/shard_map/dot_general | solution.py:171
  54.4 21.4 %collective-permute-done.5 = bf16[4,4,32,1536]{3,2,1,0:T(8,128)(2,1)S(1)} collective-permute-done((bf16[4,4,32,1536]{3,2,1,0:T(8,128)(2,1)S(1)}, bf16[4,4,32,1536]{3,2,1,0:T(8,128)(2,1)S(1)}, u32[]{:S(2)}, u32[]{:S(2)}) %collective-permute-start.5) | collective-permute-done | bytes 1572896 | tf_op jit(solution)/shard_map/ppermute | solution.py:36
  75.9 2.7 %collective-permute-done.7 = bf16[4,128,1536]{2,1,0:T(8,128)(2,1)S(1)} collective-permute-done((bf16[4,128,1536]{2,1,0:T(8,128)(2,1)S(1)}, bf16[4,128,1536]{2,1,0:T(8,128)(2,1)S(1)}, u32[]{:S(2)}, u32[]{:S(2)}) %collective-permute-start.7) | collective-permute-done | bytes 1572896 | tf_op jit(solution)/shard_map/ppermute | solution.py:36
  80.9 2.7 %collective-permute-start.10 = (bf16[2,4,32,1536]{3,2,1,0:T(8,128)(2,1)S(1)}, bf16[2,4,32,1536]{3,2,1,0:T(8,128)(2,1)S(1)}, u32[]{:S(2)}, u32[]{:S(2)}) collective-permute-start(bf16[2,4,32,1536]{3,2,1,0:T(8,128)(2,1)S(1)} %slice.51), channel_id=1, source_target_pairs={{0,3},{1,0},{2,1},{3,2},{4,7},{5,4},{6,5},{7,6},{8,11},{9,8},{10,9... | collective-permute-start | bytes 2359304 | tf_op jit(solution)/shard_map/ppermute | solution.py:41
  84.3 2.4 %collective-permute-start.12 = (bf16[2,128,1536]{2,1,0:T(8,128)(2,1)S(1)}, bf16[2,128,1536]{2,1,0:T(8,128)(2,1)S(1)}, u32[]{:S(2)}, u32[]{:S(2)}) collective-permute-start(bf16[2,128,1536]{2,1,0:T(8,128)(2,1)S(1)} %slice.53), channel_id=1, source_target_pairs={{0,96},{32,0},{64,32},{96,64},{1,97},{33,1},{65,33},{97,65},{2,98}... | collective-permute-start | bytes 2359304 | tf_op jit(solution)/shard_map/ppermute | solution.py:41
  86.7 2.6 %convolution_convert_fusion.6 = bf16[512,1536]{1,0:T(8,128)(2,1)S(1)} fusion(bf16[512,1536]{1,0:T(8,128)(2,1)S(1)} %bitcast.115, bf16[1536,1536]{1,0:T(8,128)(2,1)S(1)} %maximum_select_fusion), kind=kOutput, calls=%fused_computation.68 | convolution fusion | flops 2416705536 | bytes 7864320 | tf_op jit(solution)/shard_map/dot_general | solution.py:171
  89.3 3.7 %convolution_convert_fusion.5 = bf16[512,1536]{1,0:T(8,128)(2,1)} fusion(bf16[512,1536]{1,0:T(8,128)(2,1)S(1)} %bitcast.117, bf16[1536,1536]{1,0:T(8,128)(2,1)S(1)} %maximum_select_fusion), kind=kOutput, calls=%fused_computation.67 | convolution fusion | flops 2416705536 | bytes 7864320 | tf_op jit(solution)/shard_map/dot_general | solution.py:171
  99.8 2.6 %convolution_convert_fusion.4 = bf16[512,1536]{1,0:T(8,128)(2,1)S(1)} fusion(bf16[512,1536]{1,0:T(8,128)(2,1)S(1)} %bitcast.143, bf16[1536,1536]{1,0:T(8,128)(2,1)S(1)} %maximum_select_fusion), kind=kOutput, calls=%fused_computation.66 | convolution fusion | flops 2416705536 | bytes 7864320 | tf_op jit(solution)/shard_map/dot_general | solution.py:177
  103.7 2.7 %collective-permute-start.14 = (bf16[256,1536]{1,0:T(8,128)(2,1)}, bf16[256,1536]{1,0:T(8,128)(2,1)}, u32[]{:S(2)}, u32[]{:S(2)}) collective-permute-start(bf16[256,1536]{1,0:T(8,128)(2,1)} %get-tuple-element.139), channel_id=1, source_target_pairs={{0,3},{1,0},{2,1},{3,2},{4,7},{5,4},{6,5},{7,6},{8,11},{9,8},{10,9... | collective-permute-start | bytes 2359304 | tf_op jit(solution)/shard_map/ppermute | solution.py:219
  106.6 3.8 %convolution_convert_fusion.3 = bf16[512,1536]{1,0:T(8,128)(2,1)} fusion(bf16[512,1536]{1,0:T(8,128)(2,1)S(1)} %bitcast.146, bf16[1536,1536]{1,0:T(8,128)(2,1)S(1)} %maximum_select_fusion), kind=kOutput, calls=%fused_computation.65 | convolution fusion | flops 2416705536 | bytes 7864320 | tf_op jit(solution)/shard_map/dot_general | solution.py:177
  110.4 3.8 %convolution_convert_fusion.2 = bf16[512,1536]{1,0:T(8,128)(2,1)} fusion(bf16[512,1536]{1,0:T(8,128)(2,1)S(1)} %bitcast.145, bf16[1536,1536]{1,0:T(8,128)(2,1)S(1)} %maximum_select_fusion), kind=kOutput, calls=%fused_computation.64 | convolution fusion | flops 2416705536 | bytes 7864320 | tf_op jit(solution)/shard_map/dot_general | solution.py:177
  117.7 3.7 %convolution_convert_fusion.1 = bf16[512,1536]{1,0:T(8,128)(2,1)} fusion(bf16[512,1536]{1,0:T(8,128)(2,1)S(1)} %bitcast.130, bf16[1536,1536]{1,0:T(8,128)(2,1)S(1)} %maximum_select_fusion), kind=kOutput, calls=%fused_computation.63 | convolution fusion | flops 2416705536 | bytes 7864320 | tf_op jit(solution)/shard_map/dot_general | solution.py:171
  121.4 7.6 %all-to-all-start.1 = ((bf16[16,2,32,1536]{3,2,1,0:T(8,128)(2,1)}), bf16[16,2,32,1536]{3,2,1,0:T(8,128)(2,1)}, u32[]{:S(2)}, u32[]{:S(2)}) async-start(bf16[16,2,32,1536]{3,2,1,0:T(8,128)(2,1)} %pad_maximum_fusion), calls=%async_computation.1 | async-start | bytes 6291456 | tf_op jit(solution)/shard_map/all_to_all | solution.py:182
  130.8 4.0 %pad_maximum_fusion.1 = bf16[16,2,32,1536]{3,2,1,0:T(8,128)(2,1)} fusion(bf16[16,1,32,1536]{3,2,1,0:T(8,128)(2,1)} %bitcast.140, bf16[16,1,32,1536]{3,2,1,0:T(8,128)(2,1)} %bitcast.138), kind=kLoop, calls=%fused_computation.59 | loop fusion | flops 1572864 | bytes 6291456 | tf_op jit(solution)/shard_map/concatenate | solution.py:223
  137.8 2.9 %collective-permute-start.16 = (bf16[256,1536]{1,0:T(8,128)(2,1)S(1)}, bf16[256,1536]{1,0:T(8,128)(2,1)}, u32[]{:S(2)}, u32[]{:S(2)}) collective-permute-start(bf16[256,1536]{1,0:T(8,128)(2,1)S(1)} %fusion.30), channel_id=1, source_target_pairs={{0,3},{1,0},{2,1},{3,2},{4,7},{5,4},{6,5},{7,6},{8,11},{9,8},{10,9... | collective-permute-start | bytes 2359304 | tf_op jit(solution)/shard_map/ppermute | solution.py:230
  142.2 3.7 %convolution_convert_fusion = bf16[512,1536]{1,0:T(8,128)(2,1)} fusion(bf16[512,1536]{1,0:T(8,128)(2,1)S(1)} %bitcast.142, bf16[1536,1536]{1,0:T(8,128)(2,1)S(1)} %bitcast.129), kind=kOutput, calls=%fused_computation.62 | convolution fusion | flops 2416705536 | bytes 7864320 | tf_op jit(solution)/shard_map/dot_general | solution.py:177
  147.9 2.8 %collective-permute-done.15 = bf16[256,1536]{1,0:T(8,128)(2,1)} collective-permute-done((bf16[256,1536]{1,0:T(8,128)(2,1)S(1)}, bf16[256,1536]{1,0:T(8,128)(2,1)}, u32[]{:S(2)}, u32[]{:S(2)}) %collective-permute-start.15) | collective-permute-done | bytes 786464 | tf_op jit(solution)/shard_map/ppermute | solution.py:230
  151.2 12.8 %all-to-all-done.1 = bf16[16,2,32,1536]{3,2,1,0:T(8,128)(2,1)} async-done(((bf16[16,2,32,1536]{3,2,1,0:T(8,128)(2,1)}), bf16[16,2,32,1536]{3,2,1,0:T(8,128)(2,1)}, u32[]{:S(2)}, u32[]{:S(2)}) %all-to-all-start.1) | async-done | bytes 3145760 | tf_op jit(solution)/shard_map/all_to_all | solution.py:182
  164.0 7.7 %all-to-all-start.2 = ((bf16[16,2,32,1536]{3,2,1,0:T(8,128)(2,1)}), bf16[16,2,32,1536]{3,2,1,0:T(8,128)(2,1)}, u32[]{:S(2)}, u32[]{:S(2)}) async-start(bf16[16,2,32,1536]{3,2,1,0:T(8,128)(2,1)} %pad_maximum_fusion.1), calls=%async_computation.2 | async-start | bytes 6291456 | tf_op jit(solution)/shard_map/all_to_all | solution.py:182
  171.8 2.4 %reduce_sum.24 = bf16[2,32,1536]{2,1,0:T(8,128)(2,1)S(1)} reduce(bf16[16,2,32,1536]{3,2,1,0:T(8,128)(2,1)} %all-to-all-done.1, bf16[]{:T(256)} %constant.82.clone.1), dimensions={0}, to_apply=%region_0.1 | reduce | flops 1474560 | bytes 3342338 | tf_op jit(solution)/shard_map/reduce_sum | solution.py:261
  174.2 2.7 %collective-permute-start.18 = (bf16[256,1536]{1,0:T(8,128)(2,1)}, bf16[256,1536]{1,0:T(8,128)(2,1)S(1)}, u32[]{:S(2)}, u32[]{:S(2)}) collective-permute-start(bf16[256,1536]{1,0:T(8,128)(2,1)} %slice_bitcast_fusion), channel_id=1, source_target_pairs={{0,3},{1,0},{2,1},{3,2},{4,7},{5,4},{6,5},{7,6},{8,11},{9,8},{10,9... | collective-permute-start | bytes 2359304 | tf_op jit(solution)/shard_map/ppermute | solution.py:237
  178.5 17.8 %weight_sums.1 = (bf16[768,1536]{1,0:T(8,128)(2,1)}, bf16[768,1536]{1,0:T(8,128)(2,1)}) custom-call(s32[5]{0:T(128)S(1)} %stack.23.at_ref, bf16[512,1536]{1,0:T(8,128)(2,1)S(1)} %bitcast.114, bf16[512,1536]{1,0:T(8,128)(2,1)S(1)} %bitcast.116, bf16[512,1536]{1,0:T(8,128)(2,1)S(1)} %bitcast.118, bf16[512,1536]{1,0:T(8,128)(2,1)} %bitcast.131, ...), custom_call_target="tpu_custom_call" | custom-call | flops 9663676416 | bytes 23592960 | tf_op jit(solution)/shard_map/weight_sums/pallas_call | solution.py:124
  196.4 8.7 %collective-permute-start.20 = (bf16[768,1536]{1,0:T(8,128)(2,1)}, bf16[768,1536]{1,0:T(8,128)(2,1)}, u32[]{:S(2)}, u32[]{:S(2)}) collective-permute-start(bf16[768,1536]{1,0:T(8,128)(2,1)} %get-tuple-element.134), channel_id=1, source_target_pairs={{0,4},{4,0},{1,5},{5,1},{2,6},{6,2},{3,7},{7,3},{8,12},{12,8},{9,1... | collective-permute-start | bytes 7077896 | tf_op jit(solution)/shard_map/ppermute | solution.py:242
  207.6 2.6 %fusion.27 = bf16[4,1,128,1536]{3,2,1,0:T(8,128)(2,1)S(1)} fusion(bf16[4,1,128,1536]{3,2,1,0:T(8,128)(2,1)S(1)} %bitcast.125, bf16[4,1,128,1536]{3,2,1,0:T(8,128)(2,1)S(1)} %bitcast.126, bf16[4,1,128,1536]{3,2,1,0:T(8,128)(2,1)S(1)} %bitcast.144, bf16[4,1,128,1536]{3,2,1,0:T(8,128)(2,1)S(1)} %bitcast.127), kind=kLoop, calls=%fused_computation.56 | loop fusion | flops 19660800 | bytes 7864320 | tf_op jit(solution)/shard_map/convert_element_type | solution.py:250
  210.2 2.4 %reduce_sum.25 = bf16[2,32,1536]{2,1,0:T(8,128)(2,1)S(1)} reduce(bf16[16,2,32,1536]{3,2,1,0:T(8,128)(2,1)} %all-to-all-done.2, bf16[]{:T(256)} %constant.82.clone.1), dimensions={0}, to_apply=%region_1.2 | reduce | flops 1474560 | bytes 3342338 | tf_op jit(solution)/shard_map/reduce_sum | solution.py:261
  212.8 3.4 %collective-permute-start.19 = (bf16[4,1,128,768]{3,2,1,0:T(8,128)(2,1)S(1)}, bf16[4,1,128,768]{3,2,1,0:T(8,128)(2,1)S(1)}, u32[]{:S(2)}, u32[]{:S(2)}) collective-permute-start(bf16[4,1,128,768]{3,2,1,0:T(8,128)(2,1)S(1)} %get-tuple-element.137), channel_id=1, source_target_pairs={{0,4},{4,0},{1,5},{5,1},{2,6},{6,2},{3,7},{7,3},{8,12},{12,8},{9,1... | collective-permute-start | bytes 2359304 | tf_op jit(solution)/shard_map/ppermute | solution.py:253
  218.2 4.3 %multiply_convert_fusion = bf16[768,1536]{1,0:T(8,128)(2,1)} fusion(bf16[768,1536]{1,0:T(8,128)(2,1)} %collective-permute-done.20, bf16[768,1536]{1,0:T(8,128)(2,1)S(1)} %copy-done.9), kind=kLoop, calls=%fused_computation.28 | loop fusion | flops 5898240 | bytes 7077888 | tf_op jit(solution)/shard_map/convert_element_type | solution.py:244
  (117 shorter events, 48.9 us)
Async XLA Ops:
  4.2 13.6 %collective-permute-start = (bf16[128,1536]{1,0:T(8,128)(2,1)}, bf16[128,1536]{1,0:T(8,128)(2,1)S(1)}, u32[]{:S(2)}, u32[]{:S(2)}) collective-permute-start(bf16[128,1536]{1,0:T(8,128)(2,1)} %param.5), channel_id=1, source_target_pairs={{0,8},{8,16},{16,24},{24,0},{1,9},{9,17},{17,25},{25,1},{2,10},{10... | collective-permute-start | bytes 1179656 | tf_op jit(solution)/shard_map/ppermute | solution.py:36
  6.7 11.2 %collective-permute-start.1 = (bf16[128,1536]{1,0:T(8,128)(2,1)}, bf16[128,1536]{1,0:T(8,128)(2,1)}, u32[]{:S(2)}, u32[]{:S(2)}) collective-permute-start(bf16[128,1536]{1,0:T(8,128)(2,1)} %param.5), channel_id=1, source_target_pairs={{0,24},{8,0},{16,8},{24,16},{1,25},{9,1},{17,9},{25,17},{2,26},{10... | collective-permute-start | bytes 1179656 | tf_op jit(solution)/shard_map/ppermute | solution.py:36
  8.8 30.6 %all-to-all-start = ((bf16[16,32,1536]{2,1,0:T(8,128)(2,1)}), bf16[16,32,1536]{2,1,0:T(8,128)(2,1)S(1)}, u32[]{:S(2)}, u32[]{:S(2)}) async-start(bf16[16,32,1536]{2,1,0:T(8,128)(2,1)} %split_quarter.1), calls=%async_computation | async-start | bytes 3145728 | tf_op jit(solution)/shard_map/all_to_all | solution.py:157
  14.3 30.0 %collective-permute-start.4 = (bf16[768,1536]{1,0:T(8,128)(2,1)}, bf16[768,1536]{1,0:T(8,128)(2,1)}, u32[]{:S(2)}, u32[]{:S(2)}) collective-permute-start(bf16[768,1536]{1,0:T(8,128)(2,1)} %param.4), channel_id=1, source_target_pairs={{0,4},{4,0},{1,5},{5,1},{2,6},{6,2},{3,7},{7,3},{8,12},{12,8},{9,1... | collective-permute-start | bytes 7077896 | tf_op jit(solution)/shard_map/ppermute | solution.py:163
  17.9 21.4 %collective-permute-start.2 = (bf16[64,1536]{1,0:T(8,128)(2,1)S(1)}, bf16[64,1536]{1,0:T(8,128)(2,1)S(1)}, u32[]{:S(2)}, u32[]{:S(2)}) collective-permute-start(bf16[64,1536]{1,0:T(8,128)(2,1)S(1)} %slice.48), channel_id=1, source_target_pairs={{0,8},{8,16},{16,24},{24,0},{1,9},{9,17},{17,25},{25,1},{2,10},{10... | collective-permute-start | bytes 589832 | tf_op jit(solution)/shard_map/ppermute | solution.py:41
  19.7 19.6 %collective-permute-start.3 = (bf16[64,1536]{1,0:T(8,128)(2,1)S(1)}, bf16[64,1536]{1,0:T(8,128)(2,1)S(1)}, u32[]{:S(2)}, u32[]{:S(2)}) collective-permute-start(bf16[64,1536]{1,0:T(8,128)(2,1)S(1)} %slice.49), channel_id=1, source_target_pairs={{0,24},{8,0},{16,8},{24,16},{1,25},{9,1},{17,9},{25,17},{2,26},{10... | collective-permute-start | bytes 589832 | tf_op jit(solution)/shard_map/ppermute | solution.py:41
  39.4 7.7 %copy-start.10 = (bf16[768,1536]{1,0:T(8,128)(2,1)S(1)}, bf16[768,1536]{1,0:T(8,128)(2,1)}, u32[]{:S(2)}) copy-start(bf16[768,1536]{1,0:T(8,128)(2,1)} %param.4) | copy-start | bytes 7077892
  39.4 36.4 %collective-permute-start.5 = (bf16[4,4,32,1536]{3,2,1,0:T(8,128)(2,1)S(1)}, bf16[4,4,32,1536]{3,2,1,0:T(8,128)(2,1)S(1)}, u32[]{:S(2)}, u32[]{:S(2)}) collective-permute-start(bf16[4,4,32,1536]{3,2,1,0:T(8,128)(2,1)S(1)} %bitcast.121), channel_id=1, source_target_pairs={{0,1},{1,2},{2,3},{3,0},{4,5},{5,6},{6,7},{7,4},{8,9},{9,10},{10,1... | collective-permute-start | bytes 4718600 | tf_op jit(solution)/shard_map/ppermute | solution.py:36
  40.7 35.2 %collective-permute-start.6 = (bf16[4,4,32,1536]{3,2,1,0:T(8,128)(2,1)S(1)}, bf16[4,4,32,1536]{3,2,1,0:T(8,128)(2,1)S(1)}, u32[]{:S(2)}, u32[]{:S(2)}) collective-permute-start(bf16[4,4,32,1536]{3,2,1,0:T(8,128)(2,1)S(1)} %bitcast.122), channel_id=1, source_target_pairs={{0,3},{1,0},{2,1},{3,2},{4,7},{5,4},{6,5},{7,6},{8,11},{9,8},{10,9... | collective-permute-start | bytes 4718600 | tf_op jit(solution)/shard_map/ppermute | solution.py:36
  44.4 34.1 %collective-permute-start.7 = (bf16[4,128,1536]{2,1,0:T(8,128)(2,1)S(1)}, bf16[4,128,1536]{2,1,0:T(8,128)(2,1)S(1)}, u32[]{:S(2)}, u32[]{:S(2)}) collective-permute-start(bf16[4,128,1536]{2,1,0:T(8,128)(2,1)S(1)} %copy-done.4), channel_id=1, source_target_pairs={{0,32},{32,64},{64,96},{96,0},{1,33},{33,65},{65,97},{97,1},{2,34}... | collective-permute-start | bytes 4718600 | tf_op jit(solution)/shard_map/ppermute | solution.py:36
  45.6 32.9 %collective-permute-start.8 = (bf16[4,128,1536]{2,1,0:T(8,128)(2,1)S(1)}, bf16[4,128,1536]{2,1,0:T(8,128)(2,1)S(1)}, u32[]{:S(2)}, u32[]{:S(2)}) collective-permute-start(bf16[4,128,1536]{2,1,0:T(8,128)(2,1)S(1)} %copy-done.4), channel_id=1, source_target_pairs={{0,96},{32,0},{64,32},{96,64},{1,97},{33,1},{65,33},{97,65},{2,98}... | collective-permute-start | bytes 4718600 | tf_op jit(solution)/shard_map/ppermute | solution.py:36
  50.9 65.6 %copy-start.8 = (bf16[1536,1536]{1,0:T(8,128)(2,1)}, bf16[1536,1536]{1,0:T(8,128)(2,1)S(1)}, u32[]{:S(2)}) copy-start(bf16[1536,1536]{1,0:T(8,128)(2,1)S(1)} %maximum_select_fusion) | copy-start | bytes 14155780
  80.8 8.5 %copy-start = (bf16[4,4,32,1536]{3,2,1,0:T(8,128)(2,1)}, bf16[4,4,32,1536]{3,2,1,0:T(8,128)(2,1)S(1)}, u32[]{:S(2)}) copy-start(bf16[4,4,32,1536]{3,2,1,0:T(8,128)(2,1)S(1)} %get-tuple-element.121) | copy-start | bytes 4718596
  80.8 16.4 %collective-permute-start.9 = (bf16[2,4,32,1536]{3,2,1,0:T(8,128)(2,1)S(1)}, bf16[2,4,32,1536]{3,2,1,0:T(8,128)(2,1)S(1)}, u32[]{:S(2)}, u32[]{:S(2)}) collective-permute-start(bf16[2,4,32,1536]{3,2,1,0:T(8,128)(2,1)S(1)} %slice.50), channel_id=1, source_target_pairs={{0,1},{1,2},{2,3},{3,0},{4,5},{5,6},{6,7},{7,4},{8,9},{9,10},{10,1... | collective-permute-start | bytes 2359304 | tf_op jit(solution)/shard_map/ppermute | solution.py:41
  80.9 16.3 %collective-permute-start.10 = (bf16[2,4,32,1536]{3,2,1,0:T(8,128)(2,1)S(1)}, bf16[2,4,32,1536]{3,2,1,0:T(8,128)(2,1)S(1)}, u32[]{:S(2)}, u32[]{:S(2)}) collective-permute-start(bf16[2,4,32,1536]{3,2,1,0:T(8,128)(2,1)S(1)} %slice.51), channel_id=1, source_target_pairs={{0,3},{1,0},{2,1},{3,2},{4,7},{5,4},{6,5},{7,6},{8,11},{9,8},{10,9... | collective-permute-start | bytes 2359304 | tf_op jit(solution)/shard_map/ppermute | solution.py:41
  83.6 15.9 %collective-permute-start.11 = (bf16[2,128,1536]{2,1,0:T(8,128)(2,1)S(1)}, bf16[2,128,1536]{2,1,0:T(8,128)(2,1)S(1)}, u32[]{:S(2)}, u32[]{:S(2)}) collective-permute-start(bf16[2,128,1536]{2,1,0:T(8,128)(2,1)S(1)} %slice.52), channel_id=1, source_target_pairs={{0,32},{32,64},{64,96},{96,0},{1,33},{33,65},{65,97},{97,1},{2,34}... | collective-permute-start | bytes 2359304 | tf_op jit(solution)/shard_map/ppermute | solution.py:41
  84.3 15.2 %collective-permute-start.12 = (bf16[2,128,1536]{2,1,0:T(8,128)(2,1)S(1)}, bf16[2,128,1536]{2,1,0:T(8,128)(2,1)S(1)}, u32[]{:S(2)}, u32[]{:S(2)}) collective-permute-start(bf16[2,128,1536]{2,1,0:T(8,128)(2,1)S(1)} %slice.53), channel_id=1, source_target_pairs={{0,96},{32,0},{64,32},{96,64},{1,97},{33,1},{65,33},{97,65},{2,98}... | collective-permute-start | bytes 2359304 | tf_op jit(solution)/shard_map/ppermute | solution.py:41
  103.7 31.1 %collective-permute-start.13 = (bf16[256,1536]{1,0:T(8,128)(2,1)}, bf16[256,1536]{1,0:T(8,128)(2,1)}, u32[]{:S(2)}, u32[]{:S(2)}) collective-permute-start(bf16[256,1536]{1,0:T(8,128)(2,1)} %get-tuple-element.140), channel_id=1, source_target_pairs={{0,1},{1,2},{2,3},{3,0},{4,5},{5,6},{6,7},{7,4},{8,9},{9,10},{10,1... | collective-permute-start | bytes 2359304 | tf_op jit(solution)/shard_map/ppermute | solution.py:219
  103.7 31.1 %collective-permute-start.14 = (bf16[256,1536]{1,0:T(8,128)(2,1)}, bf16[256,1536]{1,0:T(8,128)(2,1)}, u32[]{:S(2)}, u32[]{:S(2)}) collective-permute-start(bf16[256,1536]{1,0:T(8,128)(2,1)} %get-tuple-element.139), channel_id=1, source_target_pairs={{0,3},{1,0},{2,1},{3,2},{4,7},{5,4},{6,5},{7,6},{8,11},{9,8},{10,9... | collective-permute-start | bytes 2359304 | tf_op jit(solution)/shard_map/ppermute | solution.py:219
  121.4 42.6 %all-to-all-start.1 = ((bf16[16,2,32,1536]{3,2,1,0:T(8,128)(2,1)}), bf16[16,2,32,1536]{3,2,1,0:T(8,128)(2,1)}, u32[]{:S(2)}, u32[]{:S(2)}) async-start(bf16[16,2,32,1536]{3,2,1,0:T(8,128)(2,1)} %pad_maximum_fusion), calls=%async_computation.1 | async-start | bytes 6291456 | tf_op jit(solution)/shard_map/all_to_all | solution.py:182
  130.8 11.4 %slice-start = ((s8[4718592]{0:T(1024)(128)(4,1)}), s8[4194304]{0:T(1024)(128)(4,1)S(1)}, s32[]{:S(2)}) async-start(s8[4718592]{0:T(1024)(128)(4,1)} %bitcast.128), calls=%async_computation.3 | async-start | bytes 8388608
  134.8 7.5 %slice-start.1 = ((s8[4718592]{0:T(1024)(128)(4,1)}), s8[524288]{0:T(1024)(128)(4,1)S(1)}, s32[]{:S(2)}) async-start(s8[4718592]{0:T(1024)(128)(4,1)} %bitcast.128), calls=%async_computation.4 | async-start | bytes 1048576
  136.3 14.3 %collective-permute-start.15 = (bf16[256,1536]{1,0:T(8,128)(2,1)S(1)}, bf16[256,1536]{1,0:T(8,128)(2,1)}, u32[]{:S(2)}, u32[]{:S(2)}) collective-permute-start(bf16[256,1536]{1,0:T(8,128)(2,1)S(1)} %fusion.31), channel_id=1, source_target_pairs={{0,1},{1,2},{2,3},{3,0},{4,5},{5,6},{6,7},{7,4},{8,9},{9,10},{10,1... | collective-permute-start | bytes 2359304 | tf_op jit(solution)/shard_map/ppermute | solution.py:230
  137.8 13.4 %collective-permute-start.16 = (bf16[256,1536]{1,0:T(8,128)(2,1)S(1)}, bf16[256,1536]{1,0:T(8,128)(2,1)}, u32[]{:S(2)}, u32[]{:S(2)}) collective-permute-start(bf16[256,1536]{1,0:T(8,128)(2,1)S(1)} %fusion.30), channel_id=1, source_target_pairs={{0,3},{1,0},{2,1},{3,2},{4,7},{5,4},{6,5},{7,6},{8,11},{9,8},{10,9... | collective-permute-start | bytes 2359304 | tf_op jit(solution)/shard_map/ppermute | solution.py:230
  164.0 46.2 %all-to-all-start.2 = ((bf16[16,2,32,1536]{3,2,1,0:T(8,128)(2,1)}), bf16[16,2,32,1536]{3,2,1,0:T(8,128)(2,1)}, u32[]{:S(2)}, u32[]{:S(2)}) async-start(bf16[16,2,32,1536]{3,2,1,0:T(8,128)(2,1)} %pad_maximum_fusion.1), calls=%async_computation.2 | async-start | bytes 6291456 | tf_op jit(solution)/shard_map/all_to_all | solution.py:182
  174.1 22.2 %collective-permute-start.17 = (bf16[256,1536]{1,0:T(8,128)(2,1)}, bf16[256,1536]{1,0:T(8,128)(2,1)S(1)}, u32[]{:S(2)}, u32[]{:S(2)}) collective-permute-start(bf16[256,1536]{1,0:T(8,128)(2,1)} %slice_bitcast_fusion.1), channel_id=1, source_target_pairs={{0,1},{1,2},{2,3},{3,0},{4,5},{5,6},{6,7},{7,4},{8,9},{9,10},{10,1... | collective-permute-start | bytes 2359304 | tf_op jit(solution)/shard_map/ppermute | solution.py:237
  174.2 22.1 %collective-permute-start.18 = (bf16[256,1536]{1,0:T(8,128)(2,1)}, bf16[256,1536]{1,0:T(8,128)(2,1)S(1)}, u32[]{:S(2)}, u32[]{:S(2)}) collective-permute-start(bf16[256,1536]{1,0:T(8,128)(2,1)} %slice_bitcast_fusion), channel_id=1, source_target_pairs={{0,3},{1,0},{2,1},{3,2},{4,7},{5,4},{6,5},{7,6},{8,11},{9,8},{10,9... | collective-permute-start | bytes 2359304 | tf_op jit(solution)/shard_map/ppermute | solution.py:237
  176.9 19.4 %copy-start.16 = (bf16[4,32,1536]{2,1,0:T(8,128)(2,1)}, bf16[4,32,1536]{2,1,0:T(8,128)(2,1)S(1)}, u32[]{:S(2)}) copy-start(bf16[4,32,1536]{2,1,0:T(8,128)(2,1)S(1)} %slice_dynamic-update-slice_fusion.2) | copy-start | bytes 1179652
  196.3 11.2 %copy-start.6 = (bf16[4,4,32,1536]{3,2,1,0:T(8,128)(2,1)S(1)}, bf16[4,4,32,1536]{3,2,1,0:T(8,128)(2,1)}, u32[]{:S(2)}) copy-start(bf16[4,4,32,1536]{3,2,1,0:T(8,128)(2,1)} %bitcast_dynamic-update-slice_fusion.3) | copy-start | bytes 4718596
  196.3 11.2 %copy-start.15 = (bf16[512,1536]{1,0:T(8,128)(2,1)S(1)}, bf16[512,1536]{1,0:T(8,128)(2,1)}, u32[]{:S(2)}) copy-start(bf16[512,1536]{1,0:T(8,128)(2,1)} %convolution_convert_fusion) | copy-start | bytes 4718596
  196.4 21.9 %collective-permute-start.20 = (bf16[768,1536]{1,0:T(8,128)(2,1)}, bf16[768,1536]{1,0:T(8,128)(2,1)}, u32[]{:S(2)}, u32[]{:S(2)}) collective-permute-start(bf16[768,1536]{1,0:T(8,128)(2,1)} %get-tuple-element.134), channel_id=1, source_target_pairs={{0,4},{4,0},{1,5},{5,1},{2,6},{6,2},{3,7},{7,3},{8,12},{12,8},{9,1... | collective-permute-start | bytes 7077896 | tf_op jit(solution)/shard_map/ppermute | solution.py:242
  212.8 5.3 %collective-permute-start.19 = (bf16[4,1,128,768]{3,2,1,0:T(8,128)(2,1)S(1)}, bf16[4,1,128,768]{3,2,1,0:T(8,128)(2,1)S(1)}, u32[]{:S(2)}, u32[]{:S(2)}) collective-permute-start(bf16[4,1,128,768]{3,2,1,0:T(8,128)(2,1)S(1)} %get-tuple-element.137), channel_id=1, source_target_pairs={{0,4},{4,0},{1,5},{5,1},{2,6},{6,2},{3,7},{7,3},{8,12},{12,8},{9,1... | collective-permute-start | bytes 2359304 | tf_op jit(solution)/shard_map/ppermute | solution.py:253
  (11 other events, 37.3 us)

commit v3 on v1

--- a/solution.py
+++ b/solution.py
@@ -245,16 +245,19 @@
     weight_grad = weight_grad.astype(bf16)
 
     slope = gelu_slope(rows.reshape(4 * tok, ff).astype(f32))
-    from_left = jnp.concatenate([sum_right, term_right]).astype(f32)
-    from_right = jnp.concatenate([term_left, sum_left]).astype(f32)
-    summed = home.reshape(4 * tok, ff).astype(f32) + from_left + from_right
-    grad_here, terms_b = tie((summed * slope).astype(bf16).reshape(4, 1, tok, ff), terms_b)
-    keep = lax.dynamic_slice(grad_here, (0, 0, 0, ff_dev * core), (4, 1, tok, ff_dev))
-    give = lax.dynamic_slice(grad_here, (0, 0, 0, ff_dev * (1 - core)), (4, 1, tok, ff_dev))
-    take = lax.ppermute(give, "core", SWAP)
+    sides = ((sum_right, term_left), (term_right, sum_left))
+    parts = []
+    for piece, (one, other) in enumerate(sides):
+        summed = home[piece].astype(f32) + one.astype(f32) + other.astype(f32)
+        parts.append((summed * slope[2 * tok * piece : 2 * tok * (piece + 1)]).astype(bf16).reshape(2, 1, tok, ff))
+    *parts, terms_b = tie(*parts, terms_b)
     hidden_grad = jnp.zeros((4, 2, tok, ff_dev), bf16)
-    hidden_grad = lax.dynamic_update_slice(hidden_grad, keep, (0, core, 0, 0))
-    hidden_grad = lax.dynamic_update_slice(hidden_grad, take, (0, 1 - core, 0, 0))
+    for piece, part in enumerate(parts):
+        keep = lax.dynamic_slice(part, (0, 0, 0, ff_dev * core), (2, 1, tok, ff_dev))
+        give = lax.dynamic_slice(part, (0, 0, 0, ff_dev * (1 - core)), (2, 1, tok, ff_dev))
+        take = lax.ppermute(give, "core", SWAP)
+        hidden_grad = lax.dynamic_update_slice(hidden_grad, keep, (2 * piece, core, 0, 0))
+        hidden_grad = lax.dynamic_update_slice(hidden_grad, take, (2 * piece, 1 - core, 0, 0))
     hidden_grad = hidden_grad.reshape(8 * tok, ff_dev)
 
     ffn_out = jnp.zeros((4, sub, cols), bf16)

time: 214 us -> 212 us (level)
  waiting for transfers between devices: 48.7 us -> 44.2 us
    add x0 -> x1, other arithmetic: none -> 5.03 us  [gelu_slope(): 0.5 * (1.0 + tanh_part)]
    ppermute x1, waiting for transfers between devices: 9.56 us -> 4.54 us  [body(): lax.ppermute(sum_right, 'x', RIGHT)]
    concatenate x2 -> x0, other arithmetic: 2.47 us -> none  [the longest x1 1.24 us: body(): from_left = jnp.concatenate([sum_right, term_right]).astype(f32)]
  transfers between devices with their start and end apart: 24 -> 25, of which waited for: 8 -> 9; matrix products, arithmetic and copies ran while one was open for 36% -> 37% of each run, Pallas kernels for 8% -> 8%
where the time goes in v3:
time: 212 us
  starting transfers between devices  57.4 us (27%)
  waiting for transfers between devices  44.2 us (21%)
  other arithmetic  31.4 us (15%)
  local copies, waits for them, and re-layouts  28.8 us (14%)
  matrix products  27 us (13%)
  Pallas kernels  21.6 us (10%)
    ppermute x3, waiting for transfers between devices, shift(): lax.ppermute(block, axis, RIGHT)  21 us
    pallas_call x1, Pallas kernels, weight_sums(): pl.pallas_call(weight_kernel, grid_spec=pltpu.PrefetchScalarGridSpec(num_...  18 us
    ppermute x3, waiting for transfers between devices, relay(): lax.ppermute(left[:half], axis, RIGHT)  17.1 us
    dot_general x4, matrix products, backward(): lax.dot_general(grad, weight, (((1,), (1,)), ((), ())), preferred_element...  15.4 us
    all_to_all x2, starting transfers between devices, exchange(): return lax.all_to_all(terms, plane, split_axis=0, concat_axis=0, tiled=True)  13.1 us
    dot_general x4, matrix products, forward(): out = jnp.dot(act.reshape(16 * sub, ff), weight, preferred_element_type=f32)  11.5 us
    ppermute x1, starting transfers between devices, body(): take_sum = lax.ppermute(give_sum, 'core', SWAP)  8.07 us
    ppermute x3, starting transfers between devices, relay(): lax.ppermute(right[half:], axis, LEFT)  6.97 us
  transfers between devices with their start and end apart: 25, of which 9 were waited for; matrix products, arithmetic and copies ran while one was open for 37% of the time, Pallas kernels for 8%

profile of v3, /device:TPU:1, one launch (start us, length us, event | category | flops | bytes accessed | tf_op | source)
XLA Modules:
  0.0 211.6 jit_solution(6141130264100084459)
XLA Ops:
  0.6 3.6 %split_quarter.1 = bf16[16,32,1536]{2,1,0:T(8,128)(2,1)} custom-call(s32[1]{0:T(128)} %bitcast.x_ref, bf16[128,24576]{1,0:T(8,128)(2,1)} %rows_ref.1), custom_call_target="tpu_custom_call" | custom-call | tf_op jit(solution)/shard_map/split_quarter/pallas_call | solution.py:72
  4.2 2.5 %collective-permute-start.2 = (bf16[128,1536]{1,0:T(8,128)(2,1)}, bf16[128,1536]{1,0:T(8,128)(2,1)S(1)}, u32[]{:S(2)}, u32[]{:S(2)}) collective-permute-start(bf16[128,1536]{1,0:T(8,128)(2,1)} %param.5), channel_id=1, source_target_pairs={{0,8},{8,16},{16,24},{24,0},{1,9},{9,17},{17,25},{25,1},{2,10},{10... | collective-permute-start | bytes 1179656 | tf_op jit(solution)/shard_map/ppermute | solution.py:36
  8.8 5.5 %all-to-all-start = ((bf16[16,32,1536]{2,1,0:T(8,128)(2,1)}), bf16[16,32,1536]{2,1,0:T(8,128)(2,1)S(1)}, u32[]{:S(2)}, u32[]{:S(2)}) async-start(bf16[16,32,1536]{2,1,0:T(8,128)(2,1)} %split_quarter.1), calls=%async_computation | async-start | bytes 3145728 | tf_op jit(solution)/shard_map/all_to_all | solution.py:157
  22.7 16.6 %collective-permute-done.4 = bf16[64,1536]{1,0:T(8,128)(2,1)S(1)} collective-permute-done((bf16[64,1536]{1,0:T(8,128)(2,1)S(1)}, bf16[64,1536]{1,0:T(8,128)(2,1)S(1)}, u32[]{:S(2)}, u32[]{:S(2)}) %collective-permute-start.4) | collective-permute-done | bytes 196640 | tf_op jit(solution)/shard_map/ppermute | solution.py:41
  40.7 2.3 %collective-permute-start.1 = (bf16[4,4,32,1536]{3,2,1,0:T(8,128)(2,1)S(1)}, bf16[4,4,32,1536]{3,2,1,0:T(8,128)(2,1)S(1)}, u32[]{:S(2)}, u32[]{:S(2)}) collective-permute-start(bf16[4,4,32,1536]{3,2,1,0:T(8,128)(2,1)S(1)} %bitcast.116), channel_id=1, source_target_pairs={{0,3},{1,0},{2,1},{3,2},{4,7},{5,4},{6,5},{7,6},{8,11},{9,8},{10,9... | collective-permute-start | bytes 4718600 | tf_op jit(solution)/shard_map/ppermute | solution.py:36
  48.8 3.9 %maximum_select_fusion = bf16[1536,1536]{1,0:T(8,128)(2,1)S(1)} fusion(bf16[768,1536]{1,0:T(8,128)(2,1)} %collective-permute-done.6, bf16[768,1536]{1,0:T(8,128)(2,1)S(1)} %copy-done.7, pred[]{:T(512)S(6)} %eq.3), kind=kLoop, calls=%fused_computation.27 | loop fusion | flops 21233664 | bytes 9437185 | tf_op jit(solution)/shard_map/jit(_where)/select_n | solution.py:191
  52.7 2.6 %convolution_convert_fusion.7 = bf16[512,1536]{1,0:T(8,128)(2,1)S(1)} fusion(bf16[512,1536]{1,0:T(8,128)(2,1)S(1)} %bitcast.109, bf16[1536,1536]{1,0:T(8,128)(2,1)S(1)} %maximum_select_fusion), kind=kOutput, calls=%fused_computation.65 | convolution fusion | flops 2416705536 | bytes 7864320 | tf_op jit(solution)/shard_map/dot_general | solution.py:171
  55.3 3.3 %broadcast_in_dim.61 = bf16[4,4,128,1536]{3,2,1,0:T(8,128)(2,1)} broadcast(bf16[]{:T(256)} %constant.82.clone.1), dimensions={} | broadcast | bytes 6291458 | tf_op jit(solution)/shard_map/broadcast_in_dim | solution.py:47
  59.9 15.9 %collective-permute-done = bf16[4,4,32,1536]{3,2,1,0:T(8,128)(2,1)S(1)} collective-permute-done((bf16[4,4,32,1536]{3,2,1,0:T(8,128)(2,1)S(1)}, bf16[4,4,32,1536]{3,2,1,0:T(8,128)(2,1)S(1)}, u32[]{:S(2)}, u32[]{:S(2)}) %collective-permute-start) | collective-permute-done | bytes 1572896 | tf_op jit(solution)/shard_map/ppermute | solution.py:36
  75.9 4.4 %collective-permute-done.7 = bf16[4,128,1536]{2,1,0:T(8,128)(2,1)S(1)} collective-permute-done((bf16[4,128,1536]{2,1,0:T(8,128)(2,1)S(1)}, bf16[4,128,1536]{2,1,0:T(8,128)(2,1)S(1)}, u32[]{:S(2)}, u32[]{:S(2)}) %collective-permute-start.7) | collective-permute-done | bytes 1572896 | tf_op jit(solution)/shard_map/ppermute | solution.py:36
  82.7 2.7 %collective-permute-start.10 = (bf16[2,4,32,1536]{3,2,1,0:T(8,128)(2,1)S(1)}, bf16[2,4,32,1536]{3,2,1,0:T(8,128)(2,1)}, u32[]{:S(2)}, u32[]{:S(2)}) collective-permute-start(bf16[2,4,32,1536]{3,2,1,0:T(8,128)(2,1)S(1)} %slice.63), channel_id=1, source_target_pairs={{0,3},{1,0},{2,1},{3,2},{4,7},{5,4},{6,5},{7,6},{8,11},{9,8},{10,9... | collective-permute-start | bytes 2359304 | tf_op jit(solution)/shard_map/ppermute | solution.py:41
  86.0 2.4 %collective-permute-start.12 = (bf16[2,128,1536]{2,1,0:T(8,128)(2,1)S(1)}, bf16[2,128,1536]{2,1,0:T(8,128)(2,1)S(1)}, u32[]{:S(2)}, u32[]{:S(2)}) collective-permute-start(bf16[2,128,1536]{2,1,0:T(8,128)(2,1)S(1)} %slice.65), channel_id=1, source_target_pairs={{0,96},{32,0},{64,32},{96,64},{1,97},{33,1},{65,33},{97,65},{2,98}... | collective-permute-start | bytes 2359304 | tf_op jit(solution)/shard_map/ppermute | solution.py:41
  88.5 2.6 %convolution_convert_fusion.6 = bf16[512,1536]{1,0:T(8,128)(2,1)S(1)} fusion(bf16[512,1536]{1,0:T(8,128)(2,1)S(1)} %bitcast.111, bf16[1536,1536]{1,0:T(8,128)(2,1)S(1)} %maximum_select_fusion), kind=kOutput, calls=%fused_computation.64 | convolution fusion | flops 2416705536 | bytes 7864320 | tf_op jit(solution)/shard_map/dot_general | solution.py:171
  91.1 3.7 %convolution_convert_fusion.5 = bf16[512,1536]{1,0:T(8,128)(2,1)} fusion(bf16[512,1536]{1,0:T(8,128)(2,1)S(1)} %bitcast.113, bf16[1536,1536]{1,0:T(8,128)(2,1)S(1)} %maximum_select_fusion), kind=kOutput, calls=%fused_computation.63 | convolution fusion | flops 2416705536 | bytes 7864320 | tf_op jit(solution)/shard_map/dot_general | solution.py:171
  103.2 6.7 %all-to-all-start.1 = ((bf16[16,2,32,1536]{3,2,1,0:T(8,128)(2,1)}), bf16[16,2,32,1536]{3,2,1,0:T(8,128)(2,1)}, u32[]{:S(2)}, u32[]{:S(2)}) async-start(bf16[16,2,32,1536]{3,2,1,0:T(8,128)(2,1)} %pad_maximum_fusion), calls=%async_computation.1 | async-start | bytes 6291456 | tf_op jit(solution)/shard_map/all_to_all | solution.py:182
  109.9 2.6 %fusion.29 = bf16[4,4,128,1536]{3,2,1,0:T(8,128)(2,1)} fusion(bf16[4,4,128,1536]{3,2,1,0:T(8,128)(2,1)} %bitcast_dynamic-update-slice_fusion, s32[]{:T(128)S(6)} %select_n.91, bf16[2,128,1536]{2,1,0:T(8,128)(2,1)} %copy-done.14, bf16[2,128,1536]{2,1,0:T(8,128)(2,1)} %copy-done.13), kind=kLoop, calls=%fused_computation.71 | loop fusion | flops 3145728 | bytes 3145732 | tf_op jit(solution)/shard_map/dynamic_update_slice | solution.py:51
  114.2 5.1 %convolution_convert_fusion.4 = bf16[512,1536]{1,0:T(8,128)(2,1)S(1)} fusion(bf16[512,1536]{1,0:T(8,128)(2,1)S(1)} %bitcast.137, bf16[1536,1536]{1,0:T(8,128)(2,1)} %copy-done.5), kind=kOutput, calls=%fused_computation.62 | convolution fusion | flops 2416705536 | bytes 7864320 | tf_op jit(solution)/shard_map/dot_general | solution.py:177
  119.4 2.7 %collective-permute-start.14 = (bf16[256,1536]{1,0:T(8,128)(2,1)S(1)}, bf16[256,1536]{1,0:T(8,128)(2,1)S(1)}, u32[]{:S(2)}, u32[]{:S(2)}) collective-permute-start(bf16[256,1536]{1,0:T(8,128)(2,1)S(1)} %get-tuple-element.143), channel_id=1, source_target_pairs={{0,3},{1,0},{2,1},{3,2},{4,7},{5,4},{6,5},{7,6},{8,11},{9,8},{10,9... | collective-permute-start | bytes 2359304 | tf_op jit(solution)/shard_map/ppermute | solution.py:219
  124.2 2.6 %convolution_convert_fusion.3 = bf16[512,1536]{1,0:T(8,128)(2,1)S(1)} fusion(bf16[512,1536]{1,0:T(8,128)(2,1)S(1)} %bitcast.139, bf16[1536,1536]{1,0:T(8,128)(2,1)S(1)} %bitcast.120), kind=kOutput, calls=%fused_computation.61 | convolution fusion | flops 2416705536 | bytes 7864320 | tf_op jit(solution)/shard_map/dot_general | solution.py:177
  126.9 2.6 %convolution_convert_fusion.2 = bf16[512,1536]{1,0:T(8,128)(2,1)S(1)} fusion(bf16[512,1536]{1,0:T(8,128)(2,1)S(1)} %bitcast.138, bf16[1536,1536]{1,0:T(8,128)(2,1)S(1)} %bitcast.120), kind=kOutput, calls=%fused_computation.60 | convolution fusion | flops 2416705536 | bytes 7864320 | tf_op jit(solution)/shard_map/dot_general | solution.py:177
  133.0 2.6 %convolution_convert_fusion.1 = bf16[512,1536]{1,0:T(8,128)(2,1)S(1)} fusion(bf16[512,1536]{1,0:T(8,128)(2,1)S(1)} %bitcast.124, bf16[1536,1536]{1,0:T(8,128)(2,1)S(1)} %bitcast.120), kind=kOutput, calls=%fused_computation.59 | convolution fusion | flops 2416705536 | bytes 7864320 | tf_op jit(solution)/shard_map/dot_general | solution.py:171
  138.8 2.7 %collective-permute-start.16 = (bf16[256,1536]{1,0:T(8,128)(2,1)S(1)}, bf16[256,1536]{1,0:T(8,128)(2,1)}, u32[]{:S(2)}, u32[]{:S(2)}) collective-permute-start(bf16[256,1536]{1,0:T(8,128)(2,1)S(1)} %fusion.32), channel_id=1, source_target_pairs={{0,3},{1,0},{2,1},{3,2},{4,7},{5,4},{6,5},{7,6},{8,11},{9,8},{10,9... | collective-permute-start | bytes 2359304 | tf_op jit(solution)/shard_map/ppermute | solution.py:230
  143.4 5.0 %fusion.25 = f32[512,1536]{1,0:T(8,128)} fusion(bf16[4,4,32,1536]{3,2,1,0:T(8,128)(2,1)} %bitcast_dynamic-update-slice_fusion.3), kind=kLoop, calls=%fused_computation.54 | loop fusion | flops 14155776 | bytes 4718592 | tf_op jit(solution)/shard_map/add | solution.py:19
  148.5 4.5 %collective-permute-done.15 = bf16[256,1536]{1,0:T(8,128)(2,1)} collective-permute-done((bf16[256,1536]{1,0:T(8,128)(2,1)S(1)}, bf16[256,1536]{1,0:T(8,128)(2,1)}, u32[]{:S(2)}, u32[]{:S(2)}) %collective-permute-start.15) | collective-permute-done | bytes 786464 | tf_op jit(solution)/shard_map/ppermute | solution.py:230
  153.0 6.4 %all-to-all-start.2 = ((bf16[16,2,32,1536]{3,2,1,0:T(8,128)(2,1)}), bf16[16,2,32,1536]{3,2,1,0:T(8,128)(2,1)}, u32[]{:S(2)}, u32[]{:S(2)}) async-start(bf16[16,2,32,1536]{3,2,1,0:T(8,128)(2,1)} %pad_maximum_fusion.1), calls=%async_computation.2 | async-start | bytes 6291456 | tf_op jit(solution)/shard_map/all_to_all | solution.py:182
  159.4 2.4 %reduce_sum.24 = bf16[2,32,1536]{2,1,0:T(8,128)(2,1)S(1)} reduce(bf16[16,2,32,1536]{3,2,1,0:T(8,128)(2,1)} %all-to-all-done.1, bf16[]{:T(256)} %constant.82.clone.1), dimensions={0}, to_apply=%region_0.1 | reduce | flops 1474560 | bytes 3342338 | tf_op jit(solution)/shard_map/reduce_sum | solution.py:265
  163.3 5.1 %convolution_convert_fusion = bf16[512,1536]{1,0:T(8,128)(2,1)S(1)} fusion(bf16[512,1536]{1,0:T(8,128)(2,1)S(1)} %bitcast.135, bf16[1536,1536]{1,0:T(8,128)(2,1)} %copy-done.5), kind=kOutput, calls=%fused_computation.58 | convolution fusion | flops 2416705536 | bytes 7864320 | tf_op jit(solution)/shard_map/dot_general | solution.py:177
  168.6 2.7 %collective-permute-start.18 = (bf16[256,1536]{1,0:T(8,128)(2,1)S(1)}, bf16[256,1536]{1,0:T(8,128)(2,1)S(1)}, u32[]{:S(2)}, u32[]{:S(2)}) collective-permute-start(bf16[256,1536]{1,0:T(8,128)(2,1)S(1)} %copy-done.11), channel_id=1, source_target_pairs={{0,3},{1,0},{2,1},{3,2},{4,7},{5,4},{6,5},{7,6},{8,11},{9,8},{10,9... | collective-permute-start | bytes 2359304 | tf_op jit(solution)/shard_map/ppermute | solution.py:238
  171.4 18.0 %weight_sums.1 = (bf16[768,1536]{1,0:T(8,128)(2,1)}, bf16[768,1536]{1,0:T(8,128)(2,1)}) custom-call(s32[5]{0:T(128)S(1)} %stack.23.at_ref, bf16[512,1536]{1,0:T(8,128)(2,1)S(1)} %bitcast.110, bf16[512,1536]{1,0:T(8,128)(2,1)S(1)} %bitcast.112, bf16[512,1536]{1,0:T(8,128)(2,1)S(1)} %bitcast.114, bf16[512,1536]{1,0:T(8,128)(2,1)} %bitcast.125, ...), custom_call_target="tpu_custom_call" | custom-call | flops 9663676416 | bytes 23592960 | tf_op jit(solution)/shard_map/weight_sums/pallas_call | solution.py:124
  189.4 8.1 %collective-permute-start.21 = (bf16[768,1536]{1,0:T(8,128)(2,1)}, bf16[768,1536]{1,0:T(8,128)(2,1)}, u32[]{:S(2)}, u32[]{:S(2)}) collective-permute-start(bf16[768,1536]{1,0:T(8,128)(2,1)} %get-tuple-element.138), channel_id=1, source_target_pairs={{0,4},{4,0},{1,5},{5,1},{2,6},{6,2},{3,7},{7,3},{8,12},{12,8},{9,1... | collective-permute-start | bytes 7077896 | tf_op jit(solution)/shard_map/ppermute | solution.py:243
  200.4 2.4 %reduce_sum.25 = bf16[2,32,1536]{2,1,0:T(8,128)(2,1)S(1)} reduce(bf16[16,2,32,1536]{3,2,1,0:T(8,128)(2,1)} %all-to-all-done.2, bf16[]{:T(256)} %constant.82.clone.1), dimensions={0}, to_apply=%region_1.2 | reduce | flops 1474560 | bytes 3342338 | tf_op jit(solution)/shard_map/reduce_sum | solution.py:265
  207.3 4.3 %multiply_convert_fusion = bf16[768,1536]{1,0:T(8,128)(2,1)} fusion(bf16[768,1536]{1,0:T(8,128)(2,1)} %collective-permute-done.21, bf16[768,1536]{1,0:T(8,128)(2,1)S(1)} %copy-done.6), kind=kLoop, calls=%fused_computation.28 | loop fusion | flops 5898240 | bytes 7077888 | tf_op jit(solution)/shard_map/convert_element_type | solution.py:245
  (118 shorter events, 52.1 us)
Async XLA Ops:
  4.2 13.6 %collective-permute-start.2 = (bf16[128,1536]{1,0:T(8,128)(2,1)}, bf16[128,1536]{1,0:T(8,128)(2,1)S(1)}, u32[]{:S(2)}, u32[]{:S(2)}) collective-permute-start(bf16[128,1536]{1,0:T(8,128)(2,1)} %param.5), channel_id=1, source_target_pairs={{0,8},{8,16},{16,24},{24,0},{1,9},{9,17},{17,25},{25,1},{2,10},{10... | collective-permute-start | bytes 1179656 | tf_op jit(solution)/shard_map/ppermute | solution.py:36
  6.7 11.2 %collective-permute-start.3 = (bf16[128,1536]{1,0:T(8,128)(2,1)}, bf16[128,1536]{1,0:T(8,128)(2,1)}, u32[]{:S(2)}, u32[]{:S(2)}) collective-permute-start(bf16[128,1536]{1,0:T(8,128)(2,1)} %param.5), channel_id=1, source_target_pairs={{0,24},{8,0},{16,8},{24,16},{1,25},{9,1},{17,9},{25,17},{2,26},{10... | collective-permute-start | bytes 1179656 | tf_op jit(solution)/shard_map/ppermute | solution.py:36
  8.8 30.6 %all-to-all-start = ((bf16[16,32,1536]{2,1,0:T(8,128)(2,1)}), bf16[16,32,1536]{2,1,0:T(8,128)(2,1)S(1)}, u32[]{:S(2)}, u32[]{:S(2)}) async-start(bf16[16,32,1536]{2,1,0:T(8,128)(2,1)} %split_quarter.1), calls=%async_computation | async-start | bytes 3145728 | tf_op jit(solution)/shard_map/all_to_all | solution.py:157
  14.3 31.8 %collective-permute-start.6 = (bf16[768,1536]{1,0:T(8,128)(2,1)}, bf16[768,1536]{1,0:T(8,128)(2,1)}, u32[]{:S(2)}, u32[]{:S(2)}) collective-permute-start(bf16[768,1536]{1,0:T(8,128)(2,1)} %param.4), channel_id=1, source_target_pairs={{0,4},{4,0},{1,5},{5,1},{2,6},{6,2},{3,7},{7,3},{8,12},{12,8},{9,1... | collective-permute-start | bytes 7077896 | tf_op jit(solution)/shard_map/ppermute | solution.py:163
  17.9 21.4 %collective-permute-start.4 = (bf16[64,1536]{1,0:T(8,128)(2,1)S(1)}, bf16[64,1536]{1,0:T(8,128)(2,1)S(1)}, u32[]{:S(2)}, u32[]{:S(2)}) collective-permute-start(bf16[64,1536]{1,0:T(8,128)(2,1)S(1)} %slice.60), channel_id=1, source_target_pairs={{0,8},{8,16},{16,24},{24,0},{1,9},{9,17},{17,25},{25,1},{2,10},{10... | collective-permute-start | bytes 589832 | tf_op jit(solution)/shard_map/ppermute | solution.py:41
  19.7 19.6 %collective-permute-start.5 = (bf16[64,1536]{1,0:T(8,128)(2,1)S(1)}, bf16[64,1536]{1,0:T(8,128)(2,1)S(1)}, u32[]{:S(2)}, u32[]{:S(2)}) collective-permute-start(bf16[64,1536]{1,0:T(8,128)(2,1)S(1)} %slice.61), channel_id=1, source_target_pairs={{0,24},{8,0},{16,8},{24,16},{1,25},{9,1},{17,9},{25,17},{2,26},{10... | collective-permute-start | bytes 589832 | tf_op jit(solution)/shard_map/ppermute | solution.py:41
  39.4 9.4 %copy-start.7 = (bf16[768,1536]{1,0:T(8,128)(2,1)S(1)}, bf16[768,1536]{1,0:T(8,128)(2,1)}, u32[]{:S(2)}) copy-start(bf16[768,1536]{1,0:T(8,128)(2,1)} %param.4) | copy-start | bytes 7077892
  39.4 36.4 %collective-permute-start = (bf16[4,4,32,1536]{3,2,1,0:T(8,128)(2,1)S(1)}, bf16[4,4,32,1536]{3,2,1,0:T(8,128)(2,1)S(1)}, u32[]{:S(2)}, u32[]{:S(2)}) collective-permute-start(bf16[4,4,32,1536]{3,2,1,0:T(8,128)(2,1)S(1)} %bitcast.115), channel_id=1, source_target_pairs={{0,1},{1,2},{2,3},{3,0},{4,5},{5,6},{6,7},{7,4},{8,9},{9,10},{10,1... | collective-permute-start | bytes 4718600 | tf_op jit(solution)/shard_map/ppermute | solution.py:36
  40.7 35.2 %collective-permute-start.1 = (bf16[4,4,32,1536]{3,2,1,0:T(8,128)(2,1)S(1)}, bf16[4,4,32,1536]{3,2,1,0:T(8,128)(2,1)S(1)}, u32[]{:S(2)}, u32[]{:S(2)}) collective-permute-start(bf16[4,4,32,1536]{3,2,1,0:T(8,128)(2,1)S(1)} %bitcast.116), channel_id=1, source_target_pairs={{0,3},{1,0},{2,1},{3,2},{4,7},{5,4},{6,5},{7,6},{8,11},{9,8},{10,9... | collective-permute-start | bytes 4718600 | tf_op jit(solution)/shard_map/ppermute | solution.py:36
  46.1 34.1 %collective-permute-start.7 = (bf16[4,128,1536]{2,1,0:T(8,128)(2,1)S(1)}, bf16[4,128,1536]{2,1,0:T(8,128)(2,1)S(1)}, u32[]{:S(2)}, u32[]{:S(2)}) collective-permute-start(bf16[4,128,1536]{2,1,0:T(8,128)(2,1)S(1)} %copy-done.4), channel_id=1, source_target_pairs={{0,32},{32,64},{64,96},{96,0},{1,33},{33,65},{65,97},{97,1},{2,34}... | collective-permute-start | bytes 4718600 | tf_op jit(solution)/shard_map/ppermute | solution.py:36
  47.3 32.9 %collective-permute-start.8 = (bf16[4,128,1536]{2,1,0:T(8,128)(2,1)S(1)}, bf16[4,128,1536]{2,1,0:T(8,128)(2,1)S(1)}, u32[]{:S(2)}, u32[]{:S(2)}) collective-permute-start(bf16[4,128,1536]{2,1,0:T(8,128)(2,1)S(1)} %copy-done.4), channel_id=1, source_target_pairs={{0,96},{32,0},{64,32},{96,64},{1,97},{33,1},{65,33},{97,65},{2,98}... | collective-permute-start | bytes 4718600 | tf_op jit(solution)/shard_map/ppermute | solution.py:36
  52.7 38.4 %copy-start.5 = (bf16[1536,1536]{1,0:T(8,128)(2,1)}, bf16[1536,1536]{1,0:T(8,128)(2,1)S(1)}, u32[]{:S(2)}) copy-start(bf16[1536,1536]{1,0:T(8,128)(2,1)S(1)} %maximum_select_fusion) | copy-start | bytes 14155780
  82.6 8.5 %copy-start = (bf16[4,4,32,1536]{3,2,1,0:T(8,128)(2,1)}, bf16[4,4,32,1536]{3,2,1,0:T(8,128)(2,1)S(1)}, u32[]{:S(2)}) copy-start(bf16[4,4,32,1536]{3,2,1,0:T(8,128)(2,1)S(1)} %get-tuple-element.124) | copy-start | bytes 4718596
  82.6 18.3 %collective-permute-start.9 = (bf16[2,4,32,1536]{3,2,1,0:T(8,128)(2,1)S(1)}, bf16[2,4,32,1536]{3,2,1,0:T(8,128)(2,1)}, u32[]{:S(2)}, u32[]{:S(2)}) collective-permute-start(bf16[2,4,32,1536]{3,2,1,0:T(8,128)(2,1)S(1)} %slice.62), channel_id=1, source_target_pairs={{0,1},{1,2},{2,3},{3,0},{4,5},{5,6},{6,7},{7,4},{8,9},{9,10},{10,1... | collective-permute-start | bytes 2359304 | tf_op jit(solution)/shard_map/ppermute | solution.py:41
  82.7 18.2 %collective-permute-start.10 = (bf16[2,4,32,1536]{3,2,1,0:T(8,128)(2,1)S(1)}, bf16[2,4,32,1536]{3,2,1,0:T(8,128)(2,1)}, u32[]{:S(2)}, u32[]{:S(2)}) collective-permute-start(bf16[2,4,32,1536]{3,2,1,0:T(8,128)(2,1)S(1)} %slice.63), channel_id=1, source_target_pairs={{0,3},{1,0},{2,1},{3,2},{4,7},{5,4},{6,5},{7,6},{8,11},{9,8},{10,9... | collective-permute-start | bytes 2359304 | tf_op jit(solution)/shard_map/ppermute | solution.py:41
  85.4 16.0 %collective-permute-start.11 = (bf16[2,128,1536]{2,1,0:T(8,128)(2,1)S(1)}, bf16[2,128,1536]{2,1,0:T(8,128)(2,1)S(1)}, u32[]{:S(2)}, u32[]{:S(2)}) collective-permute-start(bf16[2,128,1536]{2,1,0:T(8,128)(2,1)S(1)} %slice.64), channel_id=1, source_target_pairs={{0,32},{32,64},{64,96},{96,0},{1,33},{33,65},{65,97},{97,1},{2,34}... | collective-permute-start | bytes 2359304 | tf_op jit(solution)/shard_map/ppermute | solution.py:41
  86.0 15.3 %collective-permute-start.12 = (bf16[2,128,1536]{2,1,0:T(8,128)(2,1)S(1)}, bf16[2,128,1536]{2,1,0:T(8,128)(2,1)S(1)}, u32[]{:S(2)}, u32[]{:S(2)}) collective-permute-start(bf16[2,128,1536]{2,1,0:T(8,128)(2,1)S(1)} %slice.65), channel_id=1, source_target_pairs={{0,96},{32,0},{64,32},{96,64},{1,97},{33,1},{65,33},{97,65},{2,98}... | collective-permute-start | bytes 2359304 | tf_op jit(solution)/shard_map/ppermute | solution.py:41
  103.2 49.8 %all-to-all-start.1 = ((bf16[16,2,32,1536]{3,2,1,0:T(8,128)(2,1)}), bf16[16,2,32,1536]{3,2,1,0:T(8,128)(2,1)}, u32[]{:S(2)}, u32[]{:S(2)}) async-start(bf16[16,2,32,1536]{3,2,1,0:T(8,128)(2,1)} %pad_maximum_fusion), calls=%async_computation.1 | async-start | bytes 6291456 | tf_op jit(solution)/shard_map/all_to_all | solution.py:182
  112.5 11.7 %slice-start = ((s8[4718592]{0:T(1024)(128)(4,1)}), s8[4194304]{0:T(1024)(128)(4,1)S(1)}, s32[]{:S(2)}) async-start(s8[4718592]{0:T(1024)(128)(4,1)} %bitcast.119), calls=%async_computation.3 | async-start | bytes 8388608
  114.2 10.1 %slice-start.1 = ((s8[4718592]{0:T(1024)(128)(4,1)}), s8[524288]{0:T(1024)(128)(4,1)S(1)}, s32[]{:S(2)}) async-start(s8[4718592]{0:T(1024)(128)(4,1)} %bitcast.119), calls=%async_computation.4 | async-start | bytes 1048576
  119.4 19.0 %collective-permute-start.13 = (bf16[256,1536]{1,0:T(8,128)(2,1)S(1)}, bf16[256,1536]{1,0:T(8,128)(2,1)S(1)}, u32[]{:S(2)}, u32[]{:S(2)}) collective-permute-start(bf16[256,1536]{1,0:T(8,128)(2,1)S(1)} %get-tuple-element.144), channel_id=1, source_target_pairs={{0,1},{1,2},{2,3},{3,0},{4,5},{5,6},{6,7},{7,4},{8,9},{9,10},{10,1... | collective-permute-start | bytes 2359304 | tf_op jit(solution)/shard_map/ppermute | solution.py:219
  119.4 18.9 %collective-permute-start.14 = (bf16[256,1536]{1,0:T(8,128)(2,1)S(1)}, bf16[256,1536]{1,0:T(8,128)(2,1)S(1)}, u32[]{:S(2)}, u32[]{:S(2)}) collective-permute-start(bf16[256,1536]{1,0:T(8,128)(2,1)S(1)} %get-tuple-element.143), channel_id=1, source_target_pairs={{0,3},{1,0},{2,1},{3,2},{4,7},{5,4},{6,5},{7,6},{8,11},{9,8},{10,9... | collective-permute-start | bytes 2359304 | tf_op jit(solution)/shard_map/ppermute | solution.py:219
  138.5 14.5 %collective-permute-start.15 = (bf16[256,1536]{1,0:T(8,128)(2,1)S(1)}, bf16[256,1536]{1,0:T(8,128)(2,1)}, u32[]{:S(2)}, u32[]{:S(2)}) collective-permute-start(bf16[256,1536]{1,0:T(8,128)(2,1)S(1)} %fusion.33), channel_id=1, source_target_pairs={{0,1},{1,2},{2,3},{3,0},{4,5},{5,6},{6,7},{7,4},{8,9},{9,10},{10,1... | collective-permute-start | bytes 2359304 | tf_op jit(solution)/shard_map/ppermute | solution.py:230
  138.8 14.2 %collective-permute-start.16 = (bf16[256,1536]{1,0:T(8,128)(2,1)S(1)}, bf16[256,1536]{1,0:T(8,128)(2,1)}, u32[]{:S(2)}, u32[]{:S(2)}) collective-permute-start(bf16[256,1536]{1,0:T(8,128)(2,1)S(1)} %fusion.32), channel_id=1, source_target_pairs={{0,3},{1,0},{2,1},{3,2},{4,7},{5,4},{6,5},{7,6},{8,11},{9,8},{10,9... | collective-permute-start | bytes 2359304 | tf_op jit(solution)/shard_map/ppermute | solution.py:230
  153.0 47.4 %all-to-all-start.2 = ((bf16[16,2,32,1536]{3,2,1,0:T(8,128)(2,1)}), bf16[16,2,32,1536]{3,2,1,0:T(8,128)(2,1)}, u32[]{:S(2)}, u32[]{:S(2)}) async-start(bf16[16,2,32,1536]{3,2,1,0:T(8,128)(2,1)} %pad_maximum_fusion.1), calls=%async_computation.2 | async-start | bytes 6291456 | tf_op jit(solution)/shard_map/all_to_all | solution.py:182
  163.3 8.0 %copy-start.1 = (bf16[4,4,32,1536]{3,2,1,0:T(8,128)(2,1)S(1)}, bf16[4,4,32,1536]{3,2,1,0:T(8,128)(2,1)}, u32[]{:S(2)}) copy-start(bf16[4,4,32,1536]{3,2,1,0:T(8,128)(2,1)} %copy-done) | copy-start | bytes 4718596
  168.5 20.9 %collective-permute-start.17 = (bf16[256,1536]{1,0:T(8,128)(2,1)S(1)}, bf16[256,1536]{1,0:T(8,128)(2,1)S(1)}, u32[]{:S(2)}, u32[]{:S(2)}) collective-permute-start(bf16[256,1536]{1,0:T(8,128)(2,1)S(1)} %copy-done.12), channel_id=1, source_target_pairs={{0,1},{1,2},{2,3},{3,0},{4,5},{5,6},{6,7},{7,4},{8,9},{9,10},{10,1... | collective-permute-start | bytes 2359304 | tf_op jit(solution)/shard_map/ppermute | solution.py:238
  168.6 20.8 %collective-permute-start.18 = (bf16[256,1536]{1,0:T(8,128)(2,1)S(1)}, bf16[256,1536]{1,0:T(8,128)(2,1)S(1)}, u32[]{:S(2)}, u32[]{:S(2)}) collective-permute-start(bf16[256,1536]{1,0:T(8,128)(2,1)S(1)} %copy-done.11), channel_id=1, source_target_pairs={{0,3},{1,0},{2,1},{3,2},{4,7},{5,4},{6,5},{7,6},{8,11},{9,8},{10,9... | collective-permute-start | bytes 2359304 | tf_op jit(solution)/shard_map/ppermute | solution.py:238
  171.4 26.8 %copy-start.2 = (f32[512,1536]{1,0:T(8,128)S(1)}, f32[512,1536]{1,0:T(8,128)}, u32[]{:S(2)}) copy-start(f32[512,1536]{1,0:T(8,128)} %fusion.25) | copy-start | bytes 9437188
  189.4 17.9 %collective-permute-start.21 = (bf16[768,1536]{1,0:T(8,128)(2,1)}, bf16[768,1536]{1,0:T(8,128)(2,1)}, u32[]{:S(2)}, u32[]{:S(2)}) collective-permute-start(bf16[768,1536]{1,0:T(8,128)(2,1)} %get-tuple-element.138), channel_id=1, source_target_pairs={{0,4},{4,0},{1,5},{5,1},{2,6},{6,2},{3,7},{7,3},{8,12},{12,8},{9,1... | collective-permute-start | bytes 7077896 | tf_op jit(solution)/shard_map/ppermute | solution.py:243
  202.9 2.4 %collective-permute-start.19 = (bf16[2,1,128,768]{3,2,1,0:T(8,128)(2,1)S(1)}, bf16[2,1,128,768]{3,2,1,0:T(8,128)(2,1)S(1)}, u32[]{:S(2)}, u32[]{:S(2)}) collective-permute-start(bf16[2,1,128,768]{3,2,1,0:T(8,128)(2,1)S(1)} %get-tuple-element.147), channel_id=1, source_target_pairs={{0,4},{4,0},{1,5},{5,1},{2,6},{6,2},{3,7},{7,3},{8,12},{12,8},{9,1... | collective-permute-start | bytes 1179656 | tf_op jit(solution)/shard_map/ppermute | solution.py:258
  205.4 1.8 collective-permute-start.20
  (11 other events, 31.5 us)
